TPU v7x, 32 devices: a whole 2x2x4 slice. The times are simulated.
32 devices in a mesh: inp: 4 (over z), tm: 4 (over y, x), bl: 2 (over core).
Axes of the slice: x: 2, y: 2, z: 4, core: 2. Of those that a mesh axis runs over, the one named last changes fastest.
Arguments:
- voltages: int32 [1024, 262144], P(('inp', 'bl'), 'tm'), may hold values from -16 to 14, as said below
- taps: float32 [4, 16384], replicated, may hold values from -3 to 3
- flags: int32 [1024], P(('inp', 'bl')), may hold values 0 or 1
Outputs:
- visibilities: float32 [2, 128, 4, 256, 1024], P(None, ('inp', 'tm'), None, 'bl')
Inputs may be any that keep to these rules, and one draw needn't show every extreme that they name: `voltages`: int8-valued digitized samples, each input's stream in time order.
All inputs are finite; a program needn't handle non-finite values. No bound on the sum of `flags` on one device may be relied on, other than what follows from the above.
Results may differ from a plain program's by a relative error of at most 0.00065.
Values may be sent and summed in bfloat16 or wider, within the bound.
No kernel may reach another device: no remote copies, remote signals or barrier semaphores. Data moves between devices by JAX's collectives and lax.ppermute only.
A program may use at most 256 MiB of HBM per device.

v0:
```python
import math

import jax
import jax.numpy as jnp
from jax import lax
from jax.sharding import PartitionSpec as P

CH_AVG = 64


def passed_along(value, axis, steps):
    count = lax.axis_size(axis)
    initial, last = (max(0, -steps), min(count, count - steps))
    return lax.ppermute(value, axis, [(source, source + steps) for source in range(initial, last)])


def cos_sin(height, breadth, period):
    grid = lax.broadcasted_iota(jnp.int32, (height, breadth), 0) * lax.broadcasted_iota(
        jnp.int32, (height, breadth), 1
    )
    angle = (grid % period).astype(jnp.float32) * (2.0 * math.pi / period)
    return (jnp.cos(angle), jnp.sin(angle))


def transform(filtered, length):
    batch = filtered.shape[0]
    first_len = 128
    second_len = length // first_len
    highest = lax.Precision.HIGHEST
    blocks = filtered.reshape(batch, first_len, second_len)
    cos_one, sin_one = cos_sin(first_len, first_len, first_len)
    table_one = jnp.stack([cos_one, -sin_one])
    section_one = jnp.einsum("ykn,mnb->mykb", table_one, blocks, precision=highest)
    cos_twist, sin_twist = cos_sin(first_len, second_len, length)
    real_one = section_one[:, 0]
    imag_one = section_one[:, 1]
    twisted = jnp.stack(
        [real_one * cos_twist + imag_one * sin_twist, imag_one * cos_twist - real_one * sin_twist],
        axis=1,
    )
    cos_two, sin_two = cos_sin(second_len, second_len // 2, second_len)
    table_two = jnp.stack(
        [jnp.stack([cos_two, -sin_two], axis=1), jnp.stack([sin_two, cos_two], axis=1)]
    )
    result = jnp.einsum("mxkb,xbyq->ymqk", twisted, table_two, precision=highest)
    return result.reshape(2, batch, length // 2)


def shards(voltages, taps, flags):
    inputs = voltages.shape[0]
    tap_count = taps.shape[0]
    length = taps.shape[1]
    spectra_dev = voltages.shape[1] // length
    reach = tap_count - 1
    samples = voltages.astype(jnp.float32).reshape(inputs, spectra_dev, length)
    leading = voltages[:, : reach * length].reshape(inputs, reach, length).astype(jnp.bfloat16)
    following = passed_along(leading, "tm", -1)
    extended = jnp.concatenate([samples, following.astype(jnp.float32)], axis=1)
    filtered = jnp.zeros((inputs, spectra_dev, length), jnp.float32)
    for offset in range(tap_count):
        filtered = (
            filtered + taps[offset][None, None, :] * extended[:, offset : offset + spectra_dev]
        )
    channels = length // 2
    both_parts = transform(filtered.reshape(inputs * spectra_dev, length), length)
    scale = flags.astype(jnp.float32)[None, :, None, None] / (8.0 * math.sqrt(length))
    spectra = (both_parts.reshape(2, inputs, spectra_dev, channels) * scale).astype(jnp.bfloat16)
    turned = lax.all_to_all(
        spectra[:, None], ("inp", "tm"), split_axis=4, concat_axis=1, tiled=True
    )
    groups_inp = lax.axis_size("inp")
    groups_tm = lax.axis_size("tm")
    local_channels = channels // (groups_inp * groups_tm)
    out_groups = local_channels // CH_AVG
    rows = turned.reshape(2, groups_inp, groups_tm, inputs, spectra_dev, out_groups, CH_AVG)
    count = float(groups_tm * spectra_dev * CH_AVG)
    products = jnp.einsum(
        "xatisgk,yctjsgk->gxyaicj",
        rows,
        lax.all_gather(rows, "bl", axis=3, tiled=True),
        preferred_element_type=jnp.float32,
    )
    real_vis = products[:, 0, 0] + products[:, 1, 1]
    imag_vis = products[:, 1, 0] - products[:, 0, 1]
    visibilities = jnp.stack([real_vis, imag_vis]) / count
    return visibilities.reshape(
        2, out_groups, groups_inp, inputs, groups_inp * inputs * lax.axis_size("bl")
    )


def solution(mesh):
    in_specs = (P(("inp", "bl"), "tm"), P(), P(("inp", "bl")))
    out_specs = P(None, ("inp", "tm"), None, "bl", None)
    return jax.shard_map(shards, mesh=mesh, in_specs=in_specs, out_specs=out_specs, check_vma=False)
```

profile of v0, /device:TPU:0, one launch (start us, length us, event | category | flops | bytes accessed | tf_op | source)
XLA Modules:
  0.0 1350.8 jit_solution(1006382399046836587)
XLA Ops:
  6.5 17.0 %slice.57 = s32[128,49152]{1,0:T(8,128)} slice(s32[128,65536]{1,0:T(8,128)} %param.3), slice={[0:128], [0:49152]} | slice | bytes 50331648 | tf_op jit(solution)/shard_map/slice | solution.py:56
  23.6 24.7 %copy.82 = s32[128,49152]{0,1:T(8,128)} copy(s32[128,49152]{1,0:T(8,128)} %slice.57) | data formatting | bytes 50331648
  48.2 13.0 convert.3
  61.3 1.3 collective-permute-start
  62.6 22.5 %convert_element_type.80 = f32[128,65536]{1,0:T(8,128)} convert(s32[128,65536]{1,0:T(8,128)} %param.3) | non-fusion elementwise | flops 8388608 | bytes 67108864 | tf_op jit(solution)/shard_map/convert_element_type | solution.py:55
  85.0 33.3 %reshape.218 = f32[128,4,16384]{2,1,0:T(4,128)} reshape(f32[128,65536]{1,0:T(8,128)} %convert_element_type.80) | data formatting | bytes 67108864 | tf_op jit(solution)/shard_map/reshape | solution.py:55
  118.6 0.3 sine_negate_fusion
  119.2 0.5 convert_multiply_fusion
  119.9 216.8 %collective-permute-done = bf16[128,3,16384]{0,2,1:T(8,128)(2,1)} collective-permute-done((bf16[128,3,16384]{0,2,1:T(8,128)(2,1)}, bf16[128,3,16384]{0,2,1:T(8,128)(2,1)}, u32[]{:S(2)}, u32[]{:S(2)}) %collective-permute-start) | collective-permute-done | bytes 12582944 | tf_op jit(solution)/shard_map/ppermute | solution.py:14
  336.7 28.9 %copy.56 = f32[128,3,16384]{2,1,0:T(4,128)} copy(bf16[128,3,16384]{0,2,1:T(8,128)(2,1)} %collective-permute-done) | data formatting | bytes 37748736 | tf_op jit(solution)/shard_map/convert_element_type | solution.py:58
  365.6 90.8 %fusion.6 = f32[128,4,16384]{2,1,0:T(4,128)} fusion(f32[128,4,16384]{2,1,0:T(4,128)} %reshape.218, f32[128,3,16384]{2,1,0:T(4,128)} %copy.56, f32[16384]{0:T(1024)S(1)} %bitcast.84, f32[16384]{0:T(1024)S(1)} %bitcast.85, f32[16384]{0:T(1024)S(1)} %bitcast.83, f32[16384]{0:T(1024)S(1)} %bitcast.82), kind=kLoop, calls=%fused_computation.11 | loop fusion | flops 83886080 | bytes 92536832 | tf_op jit(solution)/shard_map/add | solution.py:62
  456.4 39.7 %reshape_reshape.6 = f32[512,128,128]{2,1,0:T(8,128)} reshape(f32[128,4,16384]{2,1,0:T(4,128)} %fusion.6) | data formatting | bytes 67108864 | tf_op jit(solution)/shard_map/reshape;reshape | solution.py:30
  496.2 59.2 %fusion.19 = f32[512,2,128,128]{2,3,1,0:T(8,128)} fusion(f32[512,128,128]{2,1,0:T(8,128)} %reshape_reshape.6, f32[1,128,128]{2,1,0:T(8,128)S(1)} %get-tuple-element.15, f32[1,128,128]{2,1,0:T(8,128)S(1)} %get-tuple-element.16), kind=kOutput, calls=%fused_computation.27 | convolution fusion | flops 25769836544 | bytes 100794368 | tf_op jit(solution)/shard_map/ykn,mnb->mykb/dot_general | solution.py:33
  555.4 43.4 %multiply_add_fusion = (f32[512,1,128,128]{2,3,1,0:T(8,128)}, f32[512,1,128,128]{2,3,1,0:T(8,128)}) fusion(f32[512,2,128,128]{2,3,1,0:T(8,128)} %fusion.19, f32[128,128]{0,1:T(8,128)S(1)} %get-tuple-element.17, f32[128,128]{0,1:T(8,128)S(1)} %get-tuple-element.18), kind=kLoop, calls=%fused_computation.25 | loop fusion | flops 50331648 | bytes 134348800 | tf_op jit(solution)/shard_map/add | solution.py:38
  598.7 44.3 %fusion.22 = f32[2,512,64,128]{3,2,1,0:T(8,128)} fusion(f32[512,1,128,128]{2,3,1,0:T(8,128)} %get-tuple-element.6, f32[512,1,128,128]{2,3,1,0:T(8,128)} %get-tuple-element.5, f32[1,128,2,64]{1,3,0,2:T(8,128)S(1)} %get-tuple-element.14, f32[1,128,2,64]{1,3,0,2:T(8,128)S(1)} %get-tuple-element.13), kind=kOutput, calls=%fused_computation.28 | convolution fusion | flops 25786613760 | bytes 100794368 | tf_op jit(solution)/shard_map/mxkb,xbyq->ymqk/dot_general | solution.py:45
  643.0 39.2 %reshape_reshape.7 = f32[2,1,128,4,8192]{4,3,2,0,1:T(4,128)} reshape(f32[2,512,64,128]{3,2,1,0:T(8,128)} %fusion.22) | data formatting | bytes 67108864 | tf_op jit(solution)/shard_map/reshape;reshape | solution.py:67
  682.2 29.7 %fusion.15 = bf16[2,1,128,4,8192]{4,2,3,1,0:T(8,128)(2,1)} fusion(f32[2,1,128,4,8192]{4,3,2,0,1:T(4,128)} %reshape_reshape.7, f32[128]{0:T(128)S(1)} %copy-done.2), kind=kLoop, calls=%fused_computation.23 | loop fusion | flops 16777216 | bytes 50332160 | tf_op jit(solution)/shard_map/convert_element_type | solution.py:67
  711.9 26.3 %copy.60 = bf16[2,1,128,4,8192]{2,3,0,1,4:T(4,128)(2,1)} copy(bf16[2,1,128,4,8192]{4,2,3,1,0:T(8,128)(2,1)} %fusion.15) | data formatting | bytes 33554432 | tf_op jit(solution)/shard_map/convert_element_type | solution.py:67
  738.2 370.5 %all_to_all.15 = bf16[2,1,128,4,8192]{2,3,0,1,4:T(4,128)(2,1)S(1)} all-to-all(bf16[2,1,128,4,8192]{2,3,0,1,4:T(4,128)(2,1)} %copy.60), channel_id=1, replica_groups=mesh['inp'=4,'tm'=4,'bl'=2] {'inp','tm'}, dimensions={4} | all-to-all | bytes 33554432 | tf_op jit(solution)/shard_map/all_to_all | solution.py:68
  1108.7 19.1 %copy.61 = bf16[2,1,128,4,8192]{2,4,3,0,1:T(8,128)(2,1)S(1)} copy(bf16[2,1,128,4,8192]{2,3,0,1,4:T(4,128)(2,1)S(1)} %all_to_all.15) | data formatting | bytes 33554432 | tf_op jit(solution)/shard_map/all_to_all | solution.py:68
  1127.8 5.7 copy-done
  1133.5 6.7 copy.63
  1140.2 50.1 %all-gather.2.cloned.1.call-done = bf16[2,4,4,256,4,8,64]{3,6,2,4,1,0,5:T(8,128)(2,1)} async-done(((bf16[2,4,4,128,4,8,64]{3,6,2,4,1,0,5:T(8,128)(2,1)}), bf16[2,4,4,256,4,8,64]{3,6,2,4,1,0,5:T(8,128)(2,1)}) %all-gather.2.cloned.1.call-update) | async-done | bytes 33554448 | tf_op jit(solution)/shard_map/all_gather | solution.py:80
  1190.3 52.2 %fusion.16 = f32[8,2,2,4,128,4,256]{4,6,3,1,5,2,0:T(8,128)} fusion(bf16[2,4,4,256,4,8,64]{3,6,2,4,1,0,5:T(8,128)(2,1)} %all-gather.2.cloned.1.call-done, bf16[2,4,4,128,4,8,64,1,1]{3,6,5,2,1,4,0,8,7:T(8,128)(2,1)} %bitcast.77), kind=kOutput, calls=%fused_computation.26 | convolution fusion | flops 34359738368 | bytes 117440512 | tf_op jit(solution)/shard_map/xatisgk,yctjsgk->gxyaicj/dot_general | solution.py:77
  1242.5 34.5 %slice_add_fusion = (f32[8,1,1,4,128,4,256]{4,6,3,1,5,2,0:T(8,128)}, f32[8,1,1,4,128,4,256]{4,6,3,1,5,2,0:T(8,128)}) fusion(f32[8,2,2,4,128,4,256]{4,6,3,1,5,2,0:T(8,128)} %fusion.16), kind=kLoop, calls=%fused_computation.30 | loop fusion | flops 8388608 | bytes 100663296 | tf_op jit(solution)/shard_map/add | solution.py:83
  1277.0 7.3 copy.65
  1284.3 0.9 slice-done.1
  1285.3 1.2 slice-done.2
  1286.5 1.2 slice-done.3
  1287.7 6.2 copy.66
  1293.9 18.2 %maximum_multiply_fusion = f32[2,8,4,128,1024]{3,4,2,1,0:T(8,128)} fusion(f32[1,8,4,128,1024]{3,4,2,1,0:T(8,128)} %bitcast.81, f32[1,8,4,128,1024]{3,4,2,1,0:T(8,128)S(1)} %bitcast.80), kind=kLoop, calls=%fused_computation.17 | loop fusion | flops 16777216 | bytes 67108864 | tf_op jit(solution)/shard_map/div | solution.py:85
  1312.0 31.9 %copy.67 = f32[2,8,4,128,1024]{4,3,2,1,0:T(8,128)} copy(f32[2,8,4,128,1024]{3,4,2,1,0:T(8,128)} %maximum_multiply_fusion) | data formatting | bytes 67108864 | tf_op jit(solution)/shard_map/div | solution.py:85
  (20 shorter events, 0.8 us)
Async XLA Ops:
  6.5 1183.8 %all-gather.2.cloned.1.call-start = ((), (), s32[]{:S(2)}) async-start(), calls=%async_computation.1 | async-start | bytes 50331648 | tf_op jit(solution)/shard_map/all_gather | solution.py:80
  61.3 275.5 %collective-permute-start = (bf16[128,3,16384]{0,2,1:T(8,128)(2,1)}, bf16[128,3,16384]{0,2,1:T(8,128)(2,1)}, u32[]{:S(2)}, u32[]{:S(2)}) collective-permute-start(bf16[128,3,16384]{0,2,1:T(8,128)(2,1)} %bitcast.7), channel_id=1, source_target_pairs={{2,0},{4,2},{6,4},{3,1},{5,3},{7,5},{10,8},{12,10},{14,12},{11,9},... | collective-permute-start | bytes 37748744 | tf_op jit(solution)/shard_map/ppermute | solution.py:14
  85.0 34.2 %copy-start.3 = (s32[128]{0:T(128)S(1)}, s32[128]{0:T(128)}, u32[]{:S(2)}) copy-start(s32[128]{0:T(128)} %param.5) | copy-start | bytes 1540
  85.0 34.7 %copy-start.1 = (f32[4,16384]{1,0:T(4,128)S(1)}, f32[4,16384]{1,0:T(4,128)}, u32[]{:S(2)}) copy-start(f32[4,16384]{1,0:T(4,128)} %param.4) | copy-start | bytes 786436
  643.0 39.2 %copy-start.2 = (f32[128]{0:T(128)S(1)}, f32[128]{0:T(128)}, u32[]{:S(2)}) copy-start(f32[128]{0:T(128)} %convert_multiply_fusion) | copy-start | bytes 1540
  1127.8 5.7 copy-start
  1277.0 7.4 slice-start
  1277.0 8.3 slice-start.1
  1277.0 9.5 slice-start.2
  1277.0 10.7 slice-start.3
Sparse Core Ops, SparseCore 0:
  1140.3 49.9 all-gather.1
where the time goes:
time: 1360 us; the launch traced here: 1350 us
  blocking collectives  371 us (27%)
  local copies, waits for them, and re-layouts  289 us (21%)
  waiting for transfers between devices  267 us (20%)
  other arithmetic  253 us (19%)
  matrix products  156 us (11%)
    all_to_all x1, blocking collectives, shards(): lax.all_to_all(spectra[:, None], ('inp', 'tm'), split_axis=4, concat_axis...  371 us
    ppermute x1, waiting for transfers between devices, passed_along(): lax.ppermute(value, axis, [(source, source + steps) for source in range(i...  217 us
    add x1, other arithmetic, shards(): filtered + taps[offset][None, None, :] * extended[:, offset:offset + spec...  90.8 us
    dot_general x1, matrix products, transform(): jnp.einsum('ykn,mnb->mykb', table_one, blocks, precision=highest)  59.2 us
    dot_general x1, matrix products, shards(): jnp.einsum('xatisgk,yctjsgk->gxyaicj', rows, lax.all_gather(rows, 'bl', a...  52.2 us
    all_gather x1, waiting for transfers between devices, shards(): lax.all_gather(rows, 'bl', axis=3, tiled=True)  50.1 us
    dot_general x1, matrix products, transform(): jnp.einsum('mxkb,xbyq->ymqk', twisted, table_two, precision=highest)  44.3 us
    add x1, other arithmetic, transform(): real_one * cos_twist + imag_one * sin_twist  43.4 us
  transfers between devices with their start and end apart: 2, of which 2 were waited for; matrix products, arithmetic and copies ran while one was open for 4% of the time, Pallas kernels for 0%

commit v1 on v0

v1 whole, which is shorter than its diff:
```python
import functools
import math

import jax
import jax.numpy as jnp
import ml_dtypes
import numpy as np
from jax import lax
from jax.experimental import pallas as pl
from jax.experimental.pallas import tpu as pltpu
from jax.sharding import PartitionSpec as P

CH_AVG = 64
LANES = 128
PAD = 136
F32 = jnp.float32
BF16 = jnp.bfloat16
VMEM_LIMIT = 56 * 1024 * 1024


def split_np(table):
    high = table.astype(np.float32).astype(ml_dtypes.bfloat16)
    low = (table - high.astype(np.float64)).astype(np.float32).astype(ml_dtypes.bfloat16)
    return high, low


def split(value):
    high = value.astype(BF16)
    return high, (value - high.astype(F32)).astype(BF16)


def angles(rows, columns, period):
    grid = np.arange(rows)[:, None] * np.arange(columns)[None, :]
    return (grid % period) * (2.0 * np.pi / period)


@functools.cache
def tables(length):
    first = angles(LANES, LANES, LANES)
    scale = 1.0 / (8.0 * math.sqrt(length))
    one = np.concatenate([np.cos(first), -np.sin(first)], axis=0) * scale
    high, low = split_np(one)
    table_one = np.concatenate(
        [
            np.concatenate([high, high], axis=1),
            np.concatenate([low, np.zeros_like(low)], axis=1),
        ],
        axis=0,
    )
    twist = angles(LANES, LANES, length)
    twists = np.stack([np.cos(twist), np.sin(twist)]).astype(np.float32)
    second = angles(LANES // 2, LANES, LANES)
    real = np.concatenate([np.cos(second), np.sin(second)], axis=1)
    imag = np.concatenate([-np.sin(second), np.cos(second)], axis=1)
    table_two = np.stack([np.stack(split_np(real)), np.stack(split_np(imag))], axis=1)
    return table_one, twists, table_two


def dft_kernel(items, length, deps, v_ref, taps_ref, flags_ref, one_ref, twist_ref, two_ref, *rest):
    outs = rest[deps:-2]
    samples, results = rest[-2:]
    rows = v_ref.shape[0]
    needed = sorted({s for item in items for _, s in item})

    @pl.loop(0, LANES, unroll=8)
    def _(n1):
        column = pl.multiple_of(n1 * LANES, LANES)
        taps = [taps_ref[k : k + 1, pl.ds(column, LANES)] for k in range(taps_ref.shape[0])]
        for part in range(rows // 8):
            v = {
                s: v_ref[part * 8 : part * 8 + 8, pl.ds(s * length + column, LANES)].astype(F32)
                for s in needed
            }
            for index, item in enumerate(items):
                total = None
                for k, s in item:
                    term = taps[k] * v[s]
                    total = term if total is None else total + term
                total = total * flags_ref[index, part * 8 : part * 8 + 8, :]
                start = (index * rows + part * 8) * PAD + n1
                samples[pl.ds(start, 8, stride=PAD), :] = total

    lower = lax.broadcasted_iota(jnp.int32, (LANES // 2, LANES), 1) < LANES // 2
    half = LANES // 2

    @pl.loop(0, len(items) * rows // 2, unroll=4)
    def _(pair):
        base = pl.multiple_of(pair * 2 * PAD, 8)
        data = jnp.concatenate(
            [samples[pl.ds(base, LANES), :], samples[pl.ds(base + PAD, LANES), :]], axis=1
        )
        high, low = split(data)
        y = jnp.dot(
            one_ref[...], jnp.concatenate([high, low], axis=0), preferred_element_type=F32
        )
        y = y[: 2 * LANES] + y[2 * LANES :]
        cos, sin = twist_ref[0], twist_ref[1]
        parts = []
        for e in range(2):
            real = y[:LANES, e * LANES : (e + 1) * LANES]
            imag = y[LANES:, e * LANES : (e + 1) * LANES]
            parts.append(
                jnp.concatenate([real * cos + imag * sin, imag * cos - real * sin], axis=1)
            )
        high, low = split(jnp.concatenate(parts, axis=0))
        dims = (((1,), (1,)), ((), ()))
        z = lax.dot_general(two_ref[...], high, dims, preferred_element_type=F32)
        z = z[:LANES] + z[LANES:]
        z = z + lax.dot_general(two_ref[:LANES, :], low, dims, preferred_element_type=F32)
        index = (pair * 2) // rows
        for e in range(2):
            row = pair * 2 + e - index * rows
            real = z[:half, e * LANES : (e + 1) * LANES]
            imag = z[half:, e * LANES : (e + 1) * LANES]
            even = jnp.where(lower, real, pltpu.roll(imag, half, 1))
            odd = jnp.where(lower, pltpu.roll(real, half, 1), imag)
            start = index * LANES * rows + row
            results[pl.ds(start, half, stride=2 * rows), :] = even
            results[pl.ds(start + rows, half, stride=2 * rows), :] = odd

    share = LANES * rows // len(outs)
    for to, out in enumerate(outs):
        for index in range(len(items)):
            chunk = results[pl.ds(index * LANES * rows + to * share, share), :]
            out[index] = chunk.astype(BF16).reshape(out.shape[1:])


def dft(items, voltages, taps, flags, one, twist, two, peers, blocks, part, parts, deps=()):
    inputs = voltages.shape[0] // parts
    length = taps.shape[1]
    rows = 16
    groups = LANES // (peers * blocks)
    count = len(items)
    whole = lambda shape: pl.BlockSpec(shape, lambda i: (0,) * len(shape))
    steps = inputs // rows
    out_shape = (count, blocks, groups, inputs, LANES)
    out_block = (count, blocks, groups, rows, LANES)
    return pl.pallas_call(
        functools.partial(dft_kernel, items, length, len(deps)),
        grid=(steps,),
        in_specs=[
            pl.BlockSpec((rows, voltages.shape[1]), lambda i: (i + part * steps, 0)),
            whole(taps.shape),
            pl.BlockSpec((count, rows, LANES), lambda i: (0, i + part * steps, 0)),
            whole(one.shape),
            whole(twist.shape),
            whole(two.shape),
        ]
        + [pl.BlockSpec(memory_space=pl.ANY)] * len(deps),
        out_specs=[pl.BlockSpec(out_block, lambda i: (0, 0, 0, i, 0))] * peers,
        out_shape=[jax.ShapeDtypeStruct(out_shape, BF16)] * peers,
        scratch_shapes=[
            pltpu.VMEM((count * rows * PAD, LANES), F32),
            pltpu.VMEM((count * rows * LANES, LANES), F32),
        ],
        compiler_params=pltpu.CompilerParams(vmem_limit_bytes=VMEM_LIMIT),
        cost_estimate=pl.CostEstimate(flops=0, bytes_accessed=1024, transcendentals=0),
        name="dft",
    )(voltages, taps, flags, one, twist, two, *deps)


def join_kernel(peers, partial, *refs):
    parts, out = refs[:peers], refs[-1]
    for e in range(peers):
        for z in range(out.shape[0]):
            value = parts[e][0, z]
            if partial:
                value = value.astype(F32) + parts[(e + 1) % peers][1, z].astype(F32)
            out[z, e] = value.astype(BF16)


def join(parts, partial, deps):
    peers = len(parts)
    count, blocks, groups, inputs, lanes = parts[0].shape
    step = inputs // 2 if inputs >= 32 else inputs
    shape = (blocks, peers, groups, inputs, lanes)
    return pl.pallas_call(
        functools.partial(join_kernel, peers, partial),
        grid=(inputs // step,),
        in_specs=[pl.BlockSpec(parts[0].shape[:3] + (step, lanes), lambda i: (0, 0, 0, i, 0))]
        * peers
        + [pl.BlockSpec(memory_space=pl.ANY)] * len(deps),
        out_specs=pl.BlockSpec(shape[:3] + (step, lanes), lambda i: (0, 0, 0, i, 0)),
        out_shape=jax.ShapeDtypeStruct(shape, BF16),
        compiler_params=pltpu.CompilerParams(vmem_limit_bytes=VMEM_LIMIT),
        cost_estimate=pl.CostEstimate(flops=10**11, bytes_accessed=1024, transcendentals=0),
        name="join",
    )(*parts, *deps)


def correlate_kernel(stages, parts, scale, add_to, place, *refs):
    count = stages * parts
    own, other = refs[:count], refs[count : 2 * count]
    rest = refs[2 * count :]
    before = rest[0] if add_to else None
    out, left, right = rest[-3:]
    blocks, times, some, lanes = own[0].shape
    inputs = some * parts
    core = place[0]
    lower = lax.broadcasted_iota(jnp.int32, (some, lanes), 1) < lanes // 2
    mine = pl.multiple_of(core * inputs, inputs)
    theirs = pl.multiple_of((1 - core) * inputs, inputs)
    for stage in range(stages):
        for part in range(parts):
            index = stage * parts + part
            row = part * some
            for z in range(blocks):
                for t in range(times):
                    column = slice((stage * times + t) * lanes, (stage * times + t + 1) * lanes)
                    tile = own[index][z, t]
                    left[z, row : row + some, column] = tile
                    turned = pltpu.roll(tile.astype(F32), lanes // 2, 1)
                    left[z, inputs + row : inputs + row + some, column] = jnp.where(
                        lower, turned, -turned
                    ).astype(BF16)
                    right[z, pl.ds(mine + row, some), column] = tile
                    right[z, pl.ds(theirs + row, some), column] = other[index][z, t]
    dims = (((1,), (1,)), ((), ()))
    for q in range(blocks):
        column = slice(q * 2 * inputs, (q + 1) * 2 * inputs)
        for a in range(blocks):
            block = lax.dot_general(left[a], right[q], dims, preferred_element_type=F32) * scale
            for part in range(2):
                value = block[part * inputs : (part + 1) * inputs]
                if add_to:
                    value = value + before[part, 0, a, :, column]
                out[part, 0, a, :, column] = value


def correlate(place, parts, own, other, scale, before=None):
    stages = len(own) // parts
    blocks, times, groups, some, lanes = own[0].shape
    inputs = some * parts
    depth = stages * times * lanes
    shape = (2, groups, blocks, inputs, 2 * blocks * inputs)
    arrays = own + other
    spec = pl.BlockSpec((blocks, times, None, some, lanes), lambda g: (0, 0, g, 0, 0))
    out_spec = pl.BlockSpec((2, 1) + shape[2:], lambda g: (0, g, 0, 0, 0))
    in_specs = [pl.BlockSpec(memory_space=pltpu.SMEM)] + [spec] * len(arrays)
    aliases = {}
    if before is not None:
        in_specs.append(out_spec)
        arrays = arrays + [before]
        aliases = {len(arrays): 0}
    return pl.pallas_call(
        functools.partial(correlate_kernel, stages, parts, scale, before is not None),
        grid=(groups,),
        in_specs=in_specs,
        out_specs=out_spec,
        out_shape=jax.ShapeDtypeStruct(shape, F32),
        scratch_shapes=[pltpu.VMEM((blocks, 2 * inputs, depth), BF16)] * 2,
        input_output_aliases=aliases,
        compiler_params=pltpu.CompilerParams(vmem_limit_bytes=VMEM_LIMIT),
        cost_estimate=pl.CostEstimate(
            flops=2 * math.prod(shape) * depth,
            bytes_accessed=math.prod(shape) * 4 * (1 if before is None else 2),
            transcendentals=0,
        ),
        name="correlate",
    )(place, *arrays)


def shift(value, axis, step):
    count = lax.axis_size(axis)
    return lax.ppermute(value, axis, [(i, (i + step) % count) for i in range(count)])


def turn(value, axis):
    return lax.all_to_all(value, axis, split_axis=0, concat_axis=0, tiled=True)


def shards(voltages, taps, flags):
    length = taps.shape[1]
    reach = taps.shape[0]
    spectra = voltages.shape[1] // length
    parts = 2
    blocks, peers = lax.axis_size("inp"), lax.axis_size("tm")
    t, core = lax.axis_index("tm"), lax.axis_index("bl")
    table_one, twists, table_two = tables(length)
    place = jnp.stack([core]).astype(jnp.int32)

    per = LANES // 2 // (blocks * peers)
    home_t = (t + jnp.arange(peers, dtype=jnp.int32)) % peers
    home_z = jnp.arange(blocks, dtype=jnp.int32)
    order = (home_z[None, :] * peers + home_t[:, None])[:, :, None] * per
    order = (order + jnp.arange(per, dtype=jnp.int32)).reshape(-1)
    two = jnp.take(jnp.asarray(table_two), order, axis=2).reshape(2 * LANES, 2 * LANES)
    one, twist = jnp.asarray(table_one), jnp.asarray(twists)

    keep = jnp.broadcast_to(flags.astype(F32)[:, None], (flags.shape[0], LANES))
    keep_two = jnp.stack([keep, keep * (t > 0).astype(F32)])

    work = [(j, part) for j in range(spectra) for part in range(parts)]
    from_dft, own, other = {}, {}, {}
    last = []

    def partial(c):
        return work[c][0] + reach > spectra

    def do_dft(c):
        j, part = work[c]
        items = [[(k, j + k) for k in range(reach) if j + k < spectra]]
        if partial(c):
            items.append([(k, j + k - spectra) for k in range(reach) if j + k >= spectra])
        sent = dft(
            items, voltages, taps, keep_two[: len(items)], one, twist, two, peers, blocks,
            part, parts, last,
        )
        last[:] = [sent[0]]
        got = {d: shift(sent[d], "tm", d) for d in range(1, peers)}
        from_dft[c] = [sent[0]] + [got[peers - e] for e in range(1, peers)]

    def do_join(c):
        early = [own[c - 2]] if c >= 2 else []
        early += [other[c - 3]] if c >= 3 else []
        sent = join(from_dft[c], partial(c), last + early)
        last[:] = [sent]
        own[c] = turn(sent, "inp")
        other[c] = shift(own[c], "bl", 1)

    count = len(work)
    for c in range(count + 1):
        if c < count:
            do_dft(c)
        if c >= 1:
            do_join(c - 1)

    def chunks(first, end):
        return [own[c] for c in range(first, end)], [other[c] for c in range(first, end)]

    scale = 1.0 / (peers * spectra * CH_AVG)
    before = correlate(place, parts, *chunks(0, count - parts), scale)
    return correlate(place, parts, *chunks(count - parts, count), scale, before)


def solution(mesh):
    in_specs = (P(("inp", "bl"), "tm"), P(), P(("inp", "bl")))
    out_specs = P(None, ("inp", "tm"), None, "bl", None)
    return jax.shard_map(shards, mesh=mesh, in_specs=in_specs, out_specs=out_specs, check_vma=False)
```

time: 1360 us -> 567 us (0.42)
  blocking collectives: 371 us -> 0 us
  Pallas kernels: 0 us -> 305 us
  local copies, waits for them, and re-layouts: 289 us -> 5.21 us
  other arithmetic: 253 us -> 2.27 us
  matrix products: 156 us -> 0 us
  waiting for transfers between devices: 267 us -> 174 us
  starting transfers between devices: 1.28 us -> 79.6 us
    all_to_all x1 -> x0, blocking collectives: 371 us -> none  [shards(): lax.all_to_all(spectra[:, None], ('inp', 'tm'), split_axis=4, concat_axis...]
    pallas_call x0 -> x18, Pallas kernels: none -> 305 us  [the longest x8 211 us: dft(): pl.pallas_call(functools.partial(dft_kernel, items, length, len(deps)), g...]
    ppermute x1 -> x32, waiting for transfers between devices: 217 us -> 4.58 us  [shift(): lax.ppermute(value, axis, [(i, (i + step) % count) for i in range(count)])]
    all_to_all x0 -> x8, waiting for transfers between devices: none -> 169 us  [turn(): return lax.all_to_all(value, axis, split_axis=0, concat_axis=0, tiled=True)]
    add x3 -> x1, other arithmetic: 169 us -> 0.07 us  [shards(): order = (order + jnp.arange(per, dtype=jnp.int32)).reshape(-1)]
    dot_general x3 -> x0, matrix products: 156 us -> none  [the longest x1 59.2 us: transform(): jnp.einsum('ykn,mnb->mykb', table_one, blocks, precision=highest)]
    another operation x2, local copies, waits for them, and re-layouts: 78.9 us -> 0.78 us  [shards(): keep_two = jnp.stack([keep, keep * (t > 0).astype(F32)])]
    convert_element_type x2 -> x0, local copies, waits for them, and re-layouts: 55.1 us -> none  [the longest x1 28.9 us: shards(): extended = jnp.concatenate([samples, following.astype(jnp.float32)], axis=1)]
  transfers between devices with their start and end apart: 2 -> 40, of which waited for: 2 -> 8; matrix products, arithmetic and copies ran while one was open for 4% -> 0% of each run, Pallas kernels for 0% -> 46%
where the time goes in v1:
time: 567 us; the launch traced here: 566 us
  Pallas kernels  305 us (54%)
  waiting for transfers between devices  174 us (31%)
  starting transfers between devices  79.6 us (14%)
    pallas_call x8, Pallas kernels, dft(): pl.pallas_call(functools.partial(dft_kernel, items, length, len(deps)), g...  211 us
    all_to_all x8, waiting for transfers between devices, turn(): return lax.all_to_all(value, axis, split_axis=0, concat_axis=0, tiled=True)  169 us
    pallas_call x2, Pallas kernels, correlate(): pl.pallas_call(functools.partial(correlate_kernel, stages, parts, scale,...  67.9 us
    ppermute x32, starting transfers between devices, shift(): lax.ppermute(value, axis, [(i, (i + step) % count) for i in range(count)])  43.7 us
    all_to_all x8, starting transfers between devices, turn(): return lax.all_to_all(value, axis, split_axis=0, concat_axis=0, tiled=True)  35.9 us
    pallas_call x8, Pallas kernels, join(): pl.pallas_call(functools.partial(join_kernel, peers, partial), grid=(inpu...  26 us
  transfers between devices with their start and end apart: 40, of which 8 were waited for; matrix products, arithmetic and copies ran while one was open for 0% of the time, Pallas kernels for 46%

profile of v1, /device:TPU:0, one launch (start us, length us, event | category | flops | bytes accessed | tf_op | source)
XLA Modules:
  0.0 565.9 jit_solution(168205562168911436)
XLA Ops:
  4.4 17.7 %dft.8 = (bf16[1,4,8,64,128]{4,3,2,1,0:T(8,128)(2,1)}, bf16[1,4,8,64,128]{4,3,2,1,0:T(8,128)(2,1)}, bf16[1,4,8,64,128]{4,3,2,1,0:T(8,128)(2,1)}, bf16[1,4,8,64,128]{4,3,2,1,0:T(8,128)(2,1)}) custom-call(s32[128,65536]{1,0:T(8,128)} %v_ref.15, f32[4,16384]{1,0:T(4,128)} %taps_ref.15, f32[1,128,128]{2,1,0:T(8,128)} %stack_broadcast_in_dim.2.flags_ref, ...), custom_call_target="tpu_custom_call" | custom-call | bytes 1024 | tf_op jit(solution)/shard_map/dft/pallas_call | solution.py:138
  22.0 3.9 collective-permute-start
  27.0 17.8 %dft.9 = (bf16[1,4,8,64,128]{4,3,2,1,0:T(8,128)(2,1)}, bf16[1,4,8,64,128]{4,3,2,1,0:T(8,128)(2,1)}, bf16[1,4,8,64,128]{4,3,2,1,0:T(8,128)(2,1)}, bf16[1,4,8,64,128]{4,3,2,1,0:T(8,128)(2,1)}) custom-call(s32[128,65536]{1,0:T(8,128)} %v_ref.15, f32[4,16384]{1,0:T(4,128)} %taps_ref.15, f32[1,128,128]{2,1,0:T(8,128)} %stack_broadcast_in_dim.2.flags_ref, ...), custom_call_target="tpu_custom_call" | custom-call | bytes 1024 | tf_op jit(solution)/shard_map/dft/pallas_call | solution.py:138
  55.4 4.9 all-to-all-start
  60.2 29.2 %dft.10 = (bf16[2,4,8,64,128]{4,3,2,1,0:T(8,128)(2,1)}, bf16[2,4,8,64,128]{4,3,2,1,0:T(8,128)(2,1)}, bf16[2,4,8,64,128]{4,3,2,1,0:T(8,128)(2,1)}, bf16[2,4,8,64,128]{4,3,2,1,0:T(8,128)(2,1)}) custom-call(s32[128,65536]{1,0:T(8,128)} %v_ref.15, f32[4,16384]{1,0:T(4,128)} %taps_ref.15, f32[2,128,128]{2,1,0:T(8,128)} %pad_maximum_fusion.flags_ref, ...), custom_call_target="tpu_custom_call" | custom-call | bytes 1024 | tf_op jit(solution)/shard_map/dft/pallas_call | solution.py:138
  89.5 10.5 %collective-permute-start.3 = (bf16[2,4,8,64,128]{4,3,2,1,0:T(8,128)(2,1)}, bf16[2,4,8,64,128]{4,3,2,1,0:T(8,128)(2,1)S(1)}, u32[]{:S(2)}, u32[]{:S(2)}) collective-permute-start(bf16[2,4,8,64,128]{4,3,2,1,0:T(8,128)(2,1)} %get-tuple-element.43), channel_id=1, source_target_pairs={{0,6},{2,0},{4,2},{6,4},{1,7},{3,1},{5,3},{7,5},{8,14},{10,8},{12,... | collective-permute-start | bytes 3145736 | tf_op jit(solution)/shard_map/ppermute | solution.py:265
  103.3 29.3 %dft.11 = (bf16[2,4,8,64,128]{4,3,2,1,0:T(8,128)(2,1)}, bf16[2,4,8,64,128]{4,3,2,1,0:T(8,128)(2,1)}, bf16[2,4,8,64,128]{4,3,2,1,0:T(8,128)(2,1)}, bf16[2,4,8,64,128]{4,3,2,1,0:T(8,128)(2,1)}) custom-call(s32[128,65536]{1,0:T(8,128)} %v_ref.15, f32[4,16384]{1,0:T(4,128)} %taps_ref.15, f32[2,128,128]{2,1,0:T(8,128)} %pad_maximum_fusion.flags_ref, ...), custom_call_target="tpu_custom_call" | custom-call | bytes 1024 | tf_op jit(solution)/shard_map/dft/pallas_call | solution.py:138
  136.9 5.1 all-to-all-start.1
  147.8 29.1 %dft.12 = (bf16[2,4,8,64,128]{4,3,2,1,0:T(8,128)(2,1)}, bf16[2,4,8,64,128]{4,3,2,1,0:T(8,128)(2,1)}, bf16[2,4,8,64,128]{4,3,2,1,0:T(8,128)(2,1)}, bf16[2,4,8,64,128]{4,3,2,1,0:T(8,128)(2,1)}) custom-call(s32[128,65536]{1,0:T(8,128)} %v_ref.15, f32[4,16384]{1,0:T(4,128)} %taps_ref.15, f32[2,128,128]{2,1,0:T(8,128)} %pad_maximum_fusion.flags_ref, ...), custom_call_target="tpu_custom_call" | custom-call | bytes 1024 | tf_op jit(solution)/shard_map/dft/pallas_call | solution.py:138
  176.9 6.4 %collective-permute-start.9 = (bf16[2,4,8,64,128]{4,3,2,1,0:T(8,128)(2,1)}, bf16[2,4,8,64,128]{4,3,2,1,0:T(8,128)(2,1)S(1)}, u32[]{:S(2)}, u32[]{:S(2)}) collective-permute-start(bf16[2,4,8,64,128]{4,3,2,1,0:T(8,128)(2,1)} %get-tuple-element.51), channel_id=1, source_target_pairs={{0,6},{2,0},{4,2},{6,4},{1,7},{3,1},{5,3},{7,5},{8,14},{10,8},{12,... | collective-permute-start | bytes 3145736 | tf_op jit(solution)/shard_map/ppermute | solution.py:265
  183.3 5.4 all-to-all-start.2
  189.6 3.5 join.11.rest_0_
  193.1 29.1 %dft.13 = (bf16[2,4,8,64,128]{4,3,2,1,0:T(8,128)(2,1)}, bf16[2,4,8,64,128]{4,3,2,1,0:T(8,128)(2,1)}, bf16[2,4,8,64,128]{4,3,2,1,0:T(8,128)(2,1)}, bf16[2,4,8,64,128]{4,3,2,1,0:T(8,128)(2,1)}) custom-call(s32[128,65536]{1,0:T(8,128)} %v_ref.15, f32[4,16384]{1,0:T(4,128)} %taps_ref.15, f32[2,128,128]{2,1,0:T(8,128)} %pad_maximum_fusion.flags_ref, ...), custom_call_target="tpu_custom_call" | custom-call | bytes 1024 | tf_op jit(solution)/shard_map/dft/pallas_call | solution.py:138
  225.0 12.4 %all-to-all-done.2.refs_5_.refs_2_ = bf16[4,4,8,64,128]{4,3,2,1,0:T(8,128)(2,1)} async-done(((bf16[4,4,8,64,128]{4,3,2,1,0:T(8,128)(2,1)}), bf16[4,4,8,64,128]{4,3,2,1,0:T(8,128)(2,1)}, u32[]{:S(2)}, u32[]{:S(2)}) %all-to-all-start.2) | async-done | bytes 2097184 | tf_op jit(solution)/shard_map/all_to_all | solution.py:269
  237.4 3.6 all-to-all-start.3
  242.0 3.4 join.12.rest_0_
  245.4 29.2 %dft.14 = (bf16[2,4,8,64,128]{4,3,2,1,0:T(8,128)(2,1)}, bf16[2,4,8,64,128]{4,3,2,1,0:T(8,128)(2,1)}, bf16[2,4,8,64,128]{4,3,2,1,0:T(8,128)(2,1)}, bf16[2,4,8,64,128]{4,3,2,1,0:T(8,128)(2,1)}) custom-call(s32[128,65536]{1,0:T(8,128)} %v_ref.15, f32[4,16384]{1,0:T(4,128)} %taps_ref.15, f32[2,128,128]{2,1,0:T(8,128)} %pad_maximum_fusion.flags_ref, ...), custom_call_target="tpu_custom_call" | custom-call | bytes 1024 | tf_op jit(solution)/shard_map/dft/pallas_call | solution.py:138
  277.4 11.3 %all-to-all-done.3.refs_5_.refs_3_ = bf16[4,4,8,64,128]{4,3,2,1,0:T(8,128)(2,1)S(1)} async-done(((bf16[4,4,8,64,128]{4,3,2,1,0:T(8,128)(2,1)}), bf16[4,4,8,64,128]{4,3,2,1,0:T(8,128)(2,1)S(1)}, u32[]{:S(2)}, u32[]{:S(2)}) %all-to-all-start.3) | async-done | bytes 2097184 | tf_op jit(solution)/shard_map/all_to_all | solution.py:269
  288.7 4.4 all-to-all-start.4
  294.4 3.5 join.13.rest_0_
  297.9 29.2 %dft.15 = (bf16[2,4,8,64,128]{4,3,2,1,0:T(8,128)(2,1)}, bf16[2,4,8,64,128]{4,3,2,1,0:T(8,128)(2,1)}, bf16[2,4,8,64,128]{4,3,2,1,0:T(8,128)(2,1)}, bf16[2,4,8,64,128]{4,3,2,1,0:T(8,128)(2,1)}) custom-call(s32[128,65536]{1,0:T(8,128)} %v_ref.15, f32[4,16384]{1,0:T(4,128)} %taps_ref.15, f32[2,128,128]{2,1,0:T(8,128)} %pad_maximum_fusion.flags_ref, ...), custom_call_target="tpu_custom_call" | custom-call | bytes 1024 | tf_op jit(solution)/shard_map/dft/pallas_call | solution.py:138
  329.7 11.3 %all-to-all-done.4.refs_5_.refs_4_ = bf16[4,4,8,64,128]{4,3,2,1,0:T(8,128)(2,1)} async-done(((bf16[4,4,8,64,128]{4,3,2,1,0:T(8,128)(2,1)}), bf16[4,4,8,64,128]{4,3,2,1,0:T(8,128)(2,1)}, u32[]{:S(2)}, u32[]{:S(2)}) %all-to-all-start.4) | async-done | bytes 2097184 | tf_op jit(solution)/shard_map/all_to_all | solution.py:269
  340.9 4.4 all-to-all-start.6
  346.6 3.4 join.14.refs_4_
  350.0 43.1 %all-to-all-done.6.refs_5_ = bf16[4,4,8,64,128]{4,3,2,1,0:T(8,128)(2,1)} async-done(((bf16[4,4,8,64,128]{4,3,2,1,0:T(8,128)(2,1)}), bf16[4,4,8,64,128]{4,3,2,1,0:T(8,128)(2,1)}, u32[]{:S(2)}, u32[]{:S(2)}) %all-to-all-start.6) | async-done | bytes 2097184 | tf_op jit(solution)/shard_map/all_to_all | solution.py:269
  393.1 3.6 all-to-all-start.5
  396.8 3.5 join.15
  400.3 44.1 %all-to-all-done.5.refs_0_ = bf16[4,4,8,64,128]{4,3,2,1,0:T(8,128)(2,1)S(1)} async-done(((bf16[4,4,8,64,128]{4,3,2,1,0:T(8,128)(2,1)}), bf16[4,4,8,64,128]{4,3,2,1,0:T(8,128)(2,1)S(1)}, u32[]{:S(2)}, u32[]{:S(2)}) %all-to-all-start.5) | async-done | bytes 2097184 | tf_op jit(solution)/shard_map/all_to_all | solution.py:269
  444.4 4.4 all-to-all-start.7
  449.4 47.2 %all-to-all-done.7.refs_1_ = bf16[4,4,8,64,128]{4,3,2,1,0:T(8,128)(2,1)} async-done(((bf16[4,4,8,64,128]{4,3,2,1,0:T(8,128)(2,1)}), bf16[4,4,8,64,128]{4,3,2,1,0:T(8,128)(2,1)}, u32[]{:S(2)}, u32[]{:S(2)}) %all-to-all-start.7) | async-done | bytes 2097184 | tf_op jit(solution)/shard_map/all_to_all | solution.py:269
  496.6 39.2 %correlate.2.refs_4_ = f32[2,8,4,128,1024]{4,3,2,1,0:T(8,128)} custom-call(s32[1]{0:T(128)} %bitcast.place, bf16[4,4,8,64,128]{4,3,2,1,0:T(8,128)(2,1)} %copy-done.2, bf16[4,4,8,64,128]{4,3,2,1,0:T(8,128)(2,1)} %all-to-all-done.1.refs_5_.refs_1_, bf16[4,4,8,64,128]{4,3,2,1,0:T(8,128)(2,1)} %all-to-all-done.2.refs_5_.refs_2_, ...), custom_call_target="tpu_custom_call" | custom-call | flops 25769803776 | bytes 33554432 | tf_op jit(solution)/shard_map/correlate/pallas_call | solution.py:245
  537.1 28.8 %correlate.3 = f32[2,8,4,128,1024]{4,3,2,1,0:T(8,128)} custom-call(s32[1]{0:T(128)} %bitcast.place, bf16[4,4,8,64,128]{4,3,2,1,0:T(8,128)(2,1)} %copy-done, bf16[4,4,8,64,128]{4,3,2,1,0:T(8,128)(2,1)} %all-to-all-done.7.refs_1_, bf16[4,4,8,64,128]{4,3,2,1,0:T(8,128)(2,1)} %collective-permute-done.29.refs_2_, ...), custom_call_target="tpu_custom_call", output_to_operand_aliasing={{}: (5, {})} | custom-call | flops 8589934592 | bytes 67108864 | tf_op jit(solution)/shard_map/correlate/pallas_call | solution.py:245
  (108 shorter events, 43.7 us)
Async XLA Ops:
  44.8 55.7 %collective-permute-start.6 = (bf16[1,4,8,64,128]{4,3,2,1,0:T(8,128)(2,1)}, bf16[1,4,8,64,128]{4,3,2,1,0:T(8,128)(2,1)}, u32[]{:S(2)}, u32[]{:S(2)}) collective-permute-start(bf16[1,4,8,64,128]{4,3,2,1,0:T(8,128)(2,1)} %get-tuple-element.46), channel_id=1, source_target_pairs={{0,6},{2,0},{4,2},{6,4},{1,7},{3,1},{5,3},{7,5},{8,14},{10,8},{12,... | collective-permute-start | bytes 1572872 | tf_op jit(solution)/shard_map/ppermute | solution.py:265
  47.1 53.4 %collective-permute-start.7 = (bf16[1,4,8,64,128]{4,3,2,1,0:T(8,128)(2,1)}, bf16[1,4,8,64,128]{4,3,2,1,0:T(8,128)(2,1)}, u32[]{:S(2)}, u32[]{:S(2)}) collective-permute-start(bf16[1,4,8,64,128]{4,3,2,1,0:T(8,128)(2,1)} %get-tuple-element.47), channel_id=1, source_target_pairs={{0,4},{2,6},{4,0},{6,2},{1,5},{3,7},{5,1},{7,3},{8,12},{10,14},{12... | collective-permute-start | bytes 1572872 | tf_op jit(solution)/shard_map/ppermute | solution.py:265
  49.4 51.2 %collective-permute-start.8 = (bf16[1,4,8,64,128]{4,3,2,1,0:T(8,128)(2,1)}, bf16[1,4,8,64,128]{4,3,2,1,0:T(8,128)(2,1)}, u32[]{:S(2)}, u32[]{:S(2)}) collective-permute-start(bf16[1,4,8,64,128]{4,3,2,1,0:T(8,128)(2,1)} %get-tuple-element.48), channel_id=1, source_target_pairs={{0,2},{2,4},{4,6},{6,0},{1,3},{3,5},{5,7},{7,1},{8,10},{10,12},{12... | collective-permute-start | bytes 1572872 | tf_op jit(solution)/shard_map/ppermute | solution.py:265
  55.4 81.5 %all-to-all-start = ((bf16[4,4,8,64,128]{4,3,2,1,0:T(8,128)(2,1)}), bf16[4,4,8,64,128]{4,3,2,1,0:T(8,128)(2,1)S(1)}, u32[]{:S(2)}, u32[]{:S(2)}) async-start(bf16[4,4,8,64,128]{4,3,2,1,0:T(8,128)(2,1)} %join.8.rest_0_), calls=%async_computation | async-start | bytes 4194304 | tf_op jit(solution)/shard_map/all_to_all | solution.py:269
  89.5 52.5 %collective-permute-start.3 = (bf16[2,4,8,64,128]{4,3,2,1,0:T(8,128)(2,1)}, bf16[2,4,8,64,128]{4,3,2,1,0:T(8,128)(2,1)S(1)}, u32[]{:S(2)}, u32[]{:S(2)}) collective-permute-start(bf16[2,4,8,64,128]{4,3,2,1,0:T(8,128)(2,1)} %get-tuple-element.43), channel_id=1, source_target_pairs={{0,6},{2,0},{4,2},{6,4},{1,7},{3,1},{5,3},{7,5},{8,14},{10,8},{12,... | collective-permute-start | bytes 3145736 | tf_op jit(solution)/shard_map/ppermute | solution.py:265
  132.6 56.1 %collective-permute-start.12 = (bf16[2,4,8,64,128]{4,3,2,1,0:T(8,128)(2,1)}, bf16[2,4,8,64,128]{4,3,2,1,0:T(8,128)(2,1)}, u32[]{:S(2)}, u32[]{:S(2)}) collective-permute-start(bf16[2,4,8,64,128]{4,3,2,1,0:T(8,128)(2,1)} %get-tuple-element.54), channel_id=1, source_target_pairs={{0,6},{2,0},{4,2},{6,4},{1,7},{3,1},{5,3},{7,5},{8,14},{10,8},{12,... | collective-permute-start | bytes 3145736 | tf_op jit(solution)/shard_map/ppermute | solution.py:265
  135.4 54.1 %collective-permute-start.13 = (bf16[2,4,8,64,128]{4,3,2,1,0:T(8,128)(2,1)}, bf16[2,4,8,64,128]{4,3,2,1,0:T(8,128)(2,1)}, u32[]{:S(2)}, u32[]{:S(2)}) collective-permute-start(bf16[2,4,8,64,128]{4,3,2,1,0:T(8,128)(2,1)} %get-tuple-element.55), channel_id=1, source_target_pairs={{0,4},{2,6},{4,0},{6,2},{1,5},{3,7},{5,1},{7,3},{8,12},{10,14},{12... | collective-permute-start | bytes 3145736 | tf_op jit(solution)/shard_map/ppermute | solution.py:265
  142.1 47.5 %collective-permute-start.15 = (bf16[4,4,8,64,128]{4,3,2,1,0:T(8,128)(2,1)S(1)}, bf16[4,4,8,64,128]{4,3,2,1,0:T(8,128)(2,1)}, u32[]{:S(2)}, u32[]{:S(2)}) collective-permute-start(bf16[4,4,8,64,128]{4,3,2,1,0:T(8,128)(2,1)S(1)} %all-to-all-done.refs_5_.refs_0_), channel_id=1, source_target_pairs={{0,1},{1,0},{2,3},{3,2},{4,5},{5,4},{6,7},{7,6},{8,9},{9,8},{10,11... | collective-permute-start | bytes 6291464 | tf_op jit(solution)/shard_map/ppermute | solution.py:265
  176.9 64.1 %collective-permute-start.9 = (bf16[2,4,8,64,128]{4,3,2,1,0:T(8,128)(2,1)}, bf16[2,4,8,64,128]{4,3,2,1,0:T(8,128)(2,1)S(1)}, u32[]{:S(2)}, u32[]{:S(2)}) collective-permute-start(bf16[2,4,8,64,128]{4,3,2,1,0:T(8,128)(2,1)} %get-tuple-element.51), channel_id=1, source_target_pairs={{0,6},{2,0},{4,2},{6,4},{1,7},{3,1},{5,3},{7,5},{8,14},{10,8},{12,... | collective-permute-start | bytes 3145736 | tf_op jit(solution)/shard_map/ppermute | solution.py:265
  183.3 54.1 %all-to-all-start.2 = ((bf16[4,4,8,64,128]{4,3,2,1,0:T(8,128)(2,1)}), bf16[4,4,8,64,128]{4,3,2,1,0:T(8,128)(2,1)}, u32[]{:S(2)}, u32[]{:S(2)}) async-start(bf16[4,4,8,64,128]{4,3,2,1,0:T(8,128)(2,1)} %join.10.rest_0_), calls=%async_computation.2 | async-start | bytes 4194304 | tf_op jit(solution)/shard_map/all_to_all | solution.py:269
  188.7 53.1 %collective-permute-start.10 = (bf16[2,4,8,64,128]{4,3,2,1,0:T(8,128)(2,1)}, bf16[2,4,8,64,128]{4,3,2,1,0:T(8,128)(2,1)}, u32[]{:S(2)}, u32[]{:S(2)}) collective-permute-start(bf16[2,4,8,64,128]{4,3,2,1,0:T(8,128)(2,1)} %get-tuple-element.52), channel_id=1, source_target_pairs={{0,4},{2,6},{4,0},{6,2},{1,5},{3,7},{5,1},{7,3},{8,12},{10,14},{12... | collective-permute-start | bytes 3145736 | tf_op jit(solution)/shard_map/ppermute | solution.py:265
  189.5 52.5 %collective-permute-start.11 = (bf16[2,4,8,64,128]{4,3,2,1,0:T(8,128)(2,1)}, bf16[2,4,8,64,128]{4,3,2,1,0:T(8,128)(2,1)}, u32[]{:S(2)}, u32[]{:S(2)}) collective-permute-start(bf16[2,4,8,64,128]{4,3,2,1,0:T(8,128)(2,1)} %get-tuple-element.53), channel_id=1, source_target_pairs={{0,2},{2,4},{4,6},{6,0},{1,3},{3,5},{5,7},{7,1},{8,10},{10,12},{12... | collective-permute-start | bytes 3145736 | tf_op jit(solution)/shard_map/ppermute | solution.py:265
  189.5 52.5 %collective-permute-start.16 = (bf16[4,4,8,64,128]{4,3,2,1,0:T(8,128)(2,1)}, bf16[4,4,8,64,128]{4,3,2,1,0:T(8,128)(2,1)}, u32[]{:S(2)}, u32[]{:S(2)}) collective-permute-start(bf16[4,4,8,64,128]{4,3,2,1,0:T(8,128)(2,1)} %all-to-all-done.1.refs_5_.refs_1_), channel_id=1, source_target_pairs={{0,1},{1,0},{2,3},{3,2},{4,5},{5,4},{6,7},{7,6},{8,9},{9,8},{10,11... | collective-permute-start | bytes 6291464 | tf_op jit(solution)/shard_map/ppermute | solution.py:265
  222.2 71.0 %collective-permute-start.20 = (bf16[2,4,8,64,128]{4,3,2,1,0:T(8,128)(2,1)}, bf16[2,4,8,64,128]{4,3,2,1,0:T(8,128)(2,1)}, u32[]{:S(2)}, u32[]{:S(2)}) collective-permute-start(bf16[2,4,8,64,128]{4,3,2,1,0:T(8,128)(2,1)} %get-tuple-element.62), channel_id=1, source_target_pairs={{0,6},{2,0},{4,2},{6,4},{1,7},{3,1},{5,3},{7,5},{8,14},{10,8},{12,... | collective-permute-start | bytes 3145736 | tf_op jit(solution)/shard_map/ppermute | solution.py:265
  237.4 51.3 %all-to-all-start.3 = ((bf16[4,4,8,64,128]{4,3,2,1,0:T(8,128)(2,1)}), bf16[4,4,8,64,128]{4,3,2,1,0:T(8,128)(2,1)S(1)}, u32[]{:S(2)}, u32[]{:S(2)}) async-start(bf16[4,4,8,64,128]{4,3,2,1,0:T(8,128)(2,1)} %join.11.rest_0_), calls=%async_computation.3 | async-start | bytes 4194304 | tf_op jit(solution)/shard_map/all_to_all | solution.py:269
  241.0 53.0 %collective-permute-start.21 = (bf16[2,4,8,64,128]{4,3,2,1,0:T(8,128)(2,1)}, bf16[2,4,8,64,128]{4,3,2,1,0:T(8,128)(2,1)}, u32[]{:S(2)}, u32[]{:S(2)}) collective-permute-start(bf16[2,4,8,64,128]{4,3,2,1,0:T(8,128)(2,1)} %get-tuple-element.63), channel_id=1, source_target_pairs={{0,4},{2,6},{4,0},{6,2},{1,5},{3,7},{5,1},{7,3},{8,12},{10,14},{12... | collective-permute-start | bytes 3145736 | tf_op jit(solution)/shard_map/ppermute | solution.py:265
  241.8 52.6 %collective-permute-start.22 = (bf16[2,4,8,64,128]{4,3,2,1,0:T(8,128)(2,1)}, bf16[2,4,8,64,128]{4,3,2,1,0:T(8,128)(2,1)}, u32[]{:S(2)}, u32[]{:S(2)}) collective-permute-start(bf16[2,4,8,64,128]{4,3,2,1,0:T(8,128)(2,1)} %get-tuple-element.64), channel_id=1, source_target_pairs={{0,2},{2,4},{4,6},{6,0},{1,3},{3,5},{5,7},{7,1},{8,10},{10,12},{12... | collective-permute-start | bytes 3145736 | tf_op jit(solution)/shard_map/ppermute | solution.py:265
  242.0 52.4 %collective-permute-start.23 = (bf16[4,4,8,64,128]{4,3,2,1,0:T(8,128)(2,1)}, bf16[4,4,8,64,128]{4,3,2,1,0:T(8,128)(2,1)}, u32[]{:S(2)}, u32[]{:S(2)}) collective-permute-start(bf16[4,4,8,64,128]{4,3,2,1,0:T(8,128)(2,1)} %all-to-all-done.2.refs_5_.refs_2_), channel_id=1, source_target_pairs={{0,1},{1,0},{2,3},{3,2},{4,5},{5,4},{6,7},{7,6},{8,9},{9,8},{10,11... | collective-permute-start | bytes 6291464 | tf_op jit(solution)/shard_map/ppermute | solution.py:265
  274.6 70.7 %collective-permute-start.17 = (bf16[2,4,8,64,128]{4,3,2,1,0:T(8,128)(2,1)}, bf16[2,4,8,64,128]{4,3,2,1,0:T(8,128)(2,1)S(1)}, u32[]{:S(2)}, u32[]{:S(2)}) collective-permute-start(bf16[2,4,8,64,128]{4,3,2,1,0:T(8,128)(2,1)} %get-tuple-element.59), channel_id=1, source_target_pairs={{0,6},{2,0},{4,2},{6,4},{1,7},{3,1},{5,3},{7,5},{8,14},{10,8},{12,... | collective-permute-start | bytes 3145736 | tf_op jit(solution)/shard_map/ppermute | solution.py:265
  288.7 52.2 %all-to-all-start.4 = ((bf16[4,4,8,64,128]{4,3,2,1,0:T(8,128)(2,1)}), bf16[4,4,8,64,128]{4,3,2,1,0:T(8,128)(2,1)}, u32[]{:S(2)}, u32[]{:S(2)}) async-start(bf16[4,4,8,64,128]{4,3,2,1,0:T(8,128)(2,1)} %join.12.rest_0_), calls=%async_computation.4 | async-start | bytes 4194304 | tf_op jit(solution)/shard_map/all_to_all | solution.py:269
  293.2 53.0 %collective-permute-start.18 = (bf16[2,4,8,64,128]{4,3,2,1,0:T(8,128)(2,1)}, bf16[2,4,8,64,128]{4,3,2,1,0:T(8,128)(2,1)}, u32[]{:S(2)}, u32[]{:S(2)}) collective-permute-start(bf16[2,4,8,64,128]{4,3,2,1,0:T(8,128)(2,1)} %get-tuple-element.60), channel_id=1, source_target_pairs={{0,4},{2,6},{4,0},{6,2},{1,5},{3,7},{5,1},{7,3},{8,12},{10,14},{12... | collective-permute-start | bytes 3145736 | tf_op jit(solution)/shard_map/ppermute | solution.py:265
  294.0 52.6 %collective-permute-start.19 = (bf16[2,4,8,64,128]{4,3,2,1,0:T(8,128)(2,1)}, bf16[2,4,8,64,128]{4,3,2,1,0:T(8,128)(2,1)}, u32[]{:S(2)}, u32[]{:S(2)}) collective-permute-start(bf16[2,4,8,64,128]{4,3,2,1,0:T(8,128)(2,1)} %get-tuple-element.61), channel_id=1, source_target_pairs={{0,2},{2,4},{4,6},{6,0},{1,3},{3,5},{5,7},{7,1},{8,10},{10,12},{12... | collective-permute-start | bytes 3145736 | tf_op jit(solution)/shard_map/ppermute | solution.py:265
  294.4 52.2 %collective-permute-start.24 = (bf16[4,4,8,64,128]{4,3,2,1,0:T(8,128)(2,1)S(1)}, bf16[4,4,8,64,128]{4,3,2,1,0:T(8,128)(2,1)}, u32[]{:S(2)}, u32[]{:S(2)}) collective-permute-start(bf16[4,4,8,64,128]{4,3,2,1,0:T(8,128)(2,1)S(1)} %all-to-all-done.3.refs_5_.refs_3_), channel_id=1, source_target_pairs={{0,1},{1,0},{2,3},{3,2},{4,5},{5,4},{6,7},{7,6},{8,9},{9,8},{10,11... | collective-permute-start | bytes 6291464 | tf_op jit(solution)/shard_map/ppermute | solution.py:265
  327.1 69.6 %collective-permute-start.25 = (bf16[2,4,8,64,128]{4,3,2,1,0:T(8,128)(2,1)}, bf16[2,4,8,64,128]{4,3,2,1,0:T(8,128)(2,1)}, u32[]{:S(2)}, u32[]{:S(2)}) collective-permute-start(bf16[2,4,8,64,128]{4,3,2,1,0:T(8,128)(2,1)} %get-tuple-element.66), channel_id=1, source_target_pairs={{0,6},{2,0},{4,2},{6,4},{1,7},{3,1},{5,3},{7,5},{8,14},{10,8},{12,... | collective-permute-start | bytes 3145736 | tf_op jit(solution)/shard_map/ppermute | solution.py:265
  340.9 52.2 %all-to-all-start.6 = ((bf16[4,4,8,64,128]{4,3,2,1,0:T(8,128)(2,1)}), bf16[4,4,8,64,128]{4,3,2,1,0:T(8,128)(2,1)}, u32[]{:S(2)}, u32[]{:S(2)}) async-start(bf16[4,4,8,64,128]{4,3,2,1,0:T(8,128)(2,1)} %join.13.rest_0_), calls=%async_computation.6 | async-start | bytes 4194304 | tf_op jit(solution)/shard_map/all_to_all | solution.py:269
  345.4 51.4 %collective-permute-start.26 = (bf16[2,4,8,64,128]{4,3,2,1,0:T(8,128)(2,1)}, bf16[2,4,8,64,128]{4,3,2,1,0:T(8,128)(2,1)}, u32[]{:S(2)}, u32[]{:S(2)}) collective-permute-start(bf16[2,4,8,64,128]{4,3,2,1,0:T(8,128)(2,1)} %get-tuple-element.67), channel_id=1, source_target_pairs={{0,4},{2,6},{4,0},{6,2},{1,5},{3,7},{5,1},{7,3},{8,12},{10,14},{12... | collective-permute-start | bytes 3145736 | tf_op jit(solution)/shard_map/ppermute | solution.py:265
  346.2 50.6 %collective-permute-start.27 = (bf16[2,4,8,64,128]{4,3,2,1,0:T(8,128)(2,1)}, bf16[2,4,8,64,128]{4,3,2,1,0:T(8,128)(2,1)}, u32[]{:S(2)}, u32[]{:S(2)}) collective-permute-start(bf16[2,4,8,64,128]{4,3,2,1,0:T(8,128)(2,1)} %get-tuple-element.68), channel_id=1, source_target_pairs={{0,2},{2,4},{4,6},{6,0},{1,3},{3,5},{5,7},{7,1},{8,10},{10,12},{12... | collective-permute-start | bytes 3145736 | tf_op jit(solution)/shard_map/ppermute | solution.py:265
  346.6 50.2 %collective-permute-start.28 = (bf16[4,4,8,64,128]{4,3,2,1,0:T(8,128)(2,1)}, bf16[4,4,8,64,128]{4,3,2,1,0:T(8,128)(2,1)}, u32[]{:S(2)}, u32[]{:S(2)}) collective-permute-start(bf16[4,4,8,64,128]{4,3,2,1,0:T(8,128)(2,1)} %all-to-all-done.4.refs_5_.refs_4_), channel_id=1, source_target_pairs={{0,1},{1,0},{2,3},{3,2},{4,5},{5,4},{6,7},{7,6},{8,9},{9,8},{10,11... | collective-permute-start | bytes 6291464 | tf_op jit(solution)/shard_map/ppermute | solution.py:265
  393.1 51.3 %all-to-all-start.5 = ((bf16[4,4,8,64,128]{4,3,2,1,0:T(8,128)(2,1)}), bf16[4,4,8,64,128]{4,3,2,1,0:T(8,128)(2,1)S(1)}, u32[]{:S(2)}, u32[]{:S(2)}) async-start(bf16[4,4,8,64,128]{4,3,2,1,0:T(8,128)(2,1)} %join.14.refs_4_), calls=%async_computation.5 | async-start | bytes 4194304 | tf_op jit(solution)/shard_map/all_to_all | solution.py:269
  444.4 52.2 %all-to-all-start.7 = ((bf16[4,4,8,64,128]{4,3,2,1,0:T(8,128)(2,1)}), bf16[4,4,8,64,128]{4,3,2,1,0:T(8,128)(2,1)}, u32[]{:S(2)}, u32[]{:S(2)}) async-start(bf16[4,4,8,64,128]{4,3,2,1,0:T(8,128)(2,1)} %join.15), calls=%async_computation.7 | async-start | bytes 4194304 | tf_op jit(solution)/shard_map/all_to_all | solution.py:269
  448.8 47.8 %collective-permute-start.31 = (bf16[4,4,8,64,128]{4,3,2,1,0:T(8,128)(2,1)}, bf16[4,4,8,64,128]{4,3,2,1,0:T(8,128)(2,1)}, u32[]{:S(2)}, u32[]{:S(2)}) collective-permute-start(bf16[4,4,8,64,128]{4,3,2,1,0:T(8,128)(2,1)} %all-to-all-done.6.refs_5_), channel_id=1, source_target_pairs={{0,1},{1,0},{2,3},{3,2},{4,5},{5,4},{6,7},{7,6},{8,9},{9,8},{10,11... | collective-permute-start | bytes 6291464 | tf_op jit(solution)/shard_map/ppermute | solution.py:265
  448.9 86.9 %collective-permute-start.29 = (bf16[4,4,8,64,128]{4,3,2,1,0:T(8,128)(2,1)S(1)}, bf16[4,4,8,64,128]{4,3,2,1,0:T(8,128)(2,1)}, u32[]{:S(2)}, u32[]{:S(2)}) collective-permute-start(bf16[4,4,8,64,128]{4,3,2,1,0:T(8,128)(2,1)S(1)} %all-to-all-done.5.refs_0_), channel_id=1, source_target_pairs={{0,1},{1,0},{2,3},{3,2},{4,5},{5,4},{6,7},{7,6},{8,9},{9,8},{10,11... | collective-permute-start | bytes 6291464 | tf_op jit(solution)/shard_map/ppermute | solution.py:265
  (20 other events, 366.4 us)

commit v2 on v1

--- a/solution.py
+++ b/solution.py
@@ -183,7 +183,7 @@
         out_specs=pl.BlockSpec(shape[:3] + (step, lanes), lambda i: (0, 0, 0, i, 0)),
         out_shape=jax.ShapeDtypeStruct(shape, BF16),
         compiler_params=pltpu.CompilerParams(vmem_limit_bytes=VMEM_LIMIT),
-        cost_estimate=pl.CostEstimate(flops=10**11, bytes_accessed=1024, transcendentals=0),
+        cost_estimate=pl.CostEstimate(flops=28 * 10**9, bytes_accessed=1024, transcendentals=0),
         name="join",
     )(*parts, *deps)
 
@@ -260,6 +260,19 @@
     )(place, *arrays)
 
 
+def after(values, dep):
+    count = len(values)
+    anywhere = pl.BlockSpec(memory_space=pl.ANY)
+    return pl.pallas_call(
+        lambda *refs: None,
+        in_specs=[anywhere] * (count + 1),
+        out_specs=[anywhere] * count,
+        out_shape=[jax.ShapeDtypeStruct(x.shape, x.dtype) for x in values],
+        input_output_aliases={i: i for i in range(count)},
+        name="after",
+    )(*values, dep)
+
+
 def shift(value, axis, step):
     count = lax.axis_size(axis)
     return lax.ppermute(value, axis, [(i, (i + step) % count) for i in range(count)])
@@ -325,12 +338,16 @@
         if c >= 1:
             do_join(c - 1)
 
-    def chunks(first, end):
-        return [own[c] for c in range(first, end)], [other[c] for c in range(first, end)]
-
     scale = 1.0 / (peers * spectra * CH_AVG)
-    before = correlate(place, parts, *chunks(0, count - parts), scale)
-    return correlate(place, parts, *chunks(count - parts, count), scale, before)
+    early, late = range(count - parts), range(count - parts, count)
+    before = correlate(
+        place, parts, [own[c] for c in early], [other[c] for c in early], scale
+    )
+    own[count - 1] = after([own[count - 1]], before)[0]
+    other[count - 1] = shift(own[count - 1], "bl", 1)
+    return correlate(
+        place, parts, [own[c] for c in late], [other[c] for c in late], scale, before
+    )
 
 
 def solution(mesh):

time: 567 us -> 506 us (0.89)
  waiting for transfers between devices: 174 us -> 121 us
  starting transfers between devices: 79.6 us -> 67.9 us
    all_to_all x8, waiting for transfers between devices: 169 us -> 89 us  [turn(): return lax.all_to_all(value, axis, split_axis=0, concat_axis=0, tiled=True)]
    ppermute x32, waiting for transfers between devices: 4.58 us -> 32.4 us  [shift(): lax.ppermute(value, axis, [(i, (i + step) % count) for i in range(count)])]
    ppermute x32, starting transfers between devices: 43.7 us -> 34.1 us  [shift(): lax.ppermute(value, axis, [(i, (i + step) % count) for i in range(count)])]
  transfers between devices with their start and end apart: 40 -> 40, of which waited for: 8 -> 12; matrix products, arithmetic and copies ran while one was open for 0% -> 0% of each run, Pallas kernels for 46% -> 51%
where the time goes in v2:
time: 506 us; the launch traced here: 505 us
  Pallas kernels  305 us (60%)
  waiting for transfers between devices  121 us (24%)
  starting transfers between devices  67.9 us (13%)
  local copies, waits for them, and re-layouts  8.79 us (2%)
    pallas_call x8, Pallas kernels, dft(): pl.pallas_call(functools.partial(dft_kernel, items, length, len(deps)), g...  211 us
    all_to_all x8, waiting for transfers between devices, turn(): return lax.all_to_all(value, axis, split_axis=0, concat_axis=0, tiled=True)  89 us
    pallas_call x2, Pallas kernels, correlate(): pl.pallas_call(functools.partial(correlate_kernel, stages, parts, scale,...  68 us
    ppermute x32, starting transfers between devices, shift(): lax.ppermute(value, axis, [(i, (i + step) % count) for i in range(count)])  34.1 us
    all_to_all x8, starting transfers between devices, turn(): return lax.all_to_all(value, axis, split_axis=0, concat_axis=0, tiled=True)  33.8 us
    ppermute x32, waiting for transfers between devices, shift(): lax.ppermute(value, axis, [(i, (i + step) % count) for i in range(count)])  32.4 us
    pallas_call x8, Pallas kernels, join(): pl.pallas_call(functools.partial(join_kernel, peers, partial), grid=(inpu...  26 us
  transfers between devices with their start and end apart: 40, of which 12 were waited for; matrix products, arithmetic and copies ran while one was open for 0% of the time, Pallas kernels for 51%

profile of v2, /device:TPU:0, one launch (start us, length us, event | category | flops | bytes accessed | tf_op | source)
XLA Modules:
  0.0 505.1 jit_solution(11367120518034658505)
XLA Ops:
  4.4 17.6 %dft.8 = (bf16[1,4,8,64,128]{4,3,2,1,0:T(8,128)(2,1)}, bf16[1,4,8,64,128]{4,3,2,1,0:T(8,128)(2,1)}, bf16[1,4,8,64,128]{4,3,2,1,0:T(8,128)(2,1)}, bf16[1,4,8,64,128]{4,3,2,1,0:T(8,128)(2,1)}) custom-call(s32[128,65536]{1,0:T(8,128)} %v_ref.15, f32[4,16384]{1,0:T(4,128)} %taps_ref.15, f32[1,128,128]{2,1,0:T(8,128)} %stack_broadcast_in_dim.2.flags_ref, ...), custom_call_target="tpu_custom_call" | custom-call | bytes 1024 | tf_op jit(solution)/shard_map/dft/pallas_call | solution.py:138
  22.0 3.9 collective-permute-start
  27.1 17.7 %dft.9 = (bf16[1,4,8,64,128]{4,3,2,1,0:T(8,128)(2,1)}, bf16[1,4,8,64,128]{4,3,2,1,0:T(8,128)(2,1)}, bf16[1,4,8,64,128]{4,3,2,1,0:T(8,128)(2,1)}, bf16[1,4,8,64,128]{4,3,2,1,0:T(8,128)(2,1)}) custom-call(s32[128,65536]{1,0:T(8,128)} %v_ref.15, f32[4,16384]{1,0:T(4,128)} %taps_ref.15, f32[1,128,128]{2,1,0:T(8,128)} %stack_broadcast_in_dim.2.flags_ref, ...), custom_call_target="tpu_custom_call" | custom-call | bytes 1024 | tf_op jit(solution)/shard_map/dft/pallas_call | solution.py:138
  55.4 5.0 all-to-all-start
  61.1 29.3 %dft.10 = (bf16[2,4,8,64,128]{4,3,2,1,0:T(8,128)(2,1)}, bf16[2,4,8,64,128]{4,3,2,1,0:T(8,128)(2,1)}, bf16[2,4,8,64,128]{4,3,2,1,0:T(8,128)(2,1)}, bf16[2,4,8,64,128]{4,3,2,1,0:T(8,128)(2,1)}) custom-call(s32[128,65536]{1,0:T(8,128)} %v_ref.15, f32[4,16384]{1,0:T(4,128)} %taps_ref.15, f32[2,128,128]{2,1,0:T(8,128)} %pad_maximum_fusion.flags_ref, ...), custom_call_target="tpu_custom_call" | custom-call | bytes 1024 | tf_op jit(solution)/shard_map/dft/pallas_call | solution.py:138
  90.4 10.5 %collective-permute-start.3 = (bf16[2,4,8,64,128]{4,3,2,1,0:T(8,128)(2,1)}, bf16[2,4,8,64,128]{4,3,2,1,0:T(8,128)(2,1)S(1)}, u32[]{:S(2)}, u32[]{:S(2)}) collective-permute-start(bf16[2,4,8,64,128]{4,3,2,1,0:T(8,128)(2,1)} %get-tuple-element.43), channel_id=1, source_target_pairs={{0,6},{2,0},{4,2},{6,4},{1,7},{3,1},{5,3},{7,5},{8,14},{10,8},{12,... | collective-permute-start | bytes 3145736 | tf_op jit(solution)/shard_map/ppermute | solution.py:278
  105.3 4.5 all-to-all-start.1
  109.8 29.3 %dft.11 = (bf16[2,4,8,64,128]{4,3,2,1,0:T(8,128)(2,1)}, bf16[2,4,8,64,128]{4,3,2,1,0:T(8,128)(2,1)}, bf16[2,4,8,64,128]{4,3,2,1,0:T(8,128)(2,1)}, bf16[2,4,8,64,128]{4,3,2,1,0:T(8,128)(2,1)}) custom-call(s32[128,65536]{1,0:T(8,128)} %v_ref.15, f32[4,16384]{1,0:T(4,128)} %taps_ref.15, f32[2,128,128]{2,1,0:T(8,128)} %pad_maximum_fusion.flags_ref, ...), custom_call_target="tpu_custom_call" | custom-call | bytes 1024 | tf_op jit(solution)/shard_map/dft/pallas_call | solution.py:138
  147.3 10.3 %all-to-all-done.1.refs_5_.refs_1_ = bf16[4,4,8,64,128]{4,3,2,1,0:T(8,128)(2,1)} async-done(((bf16[4,4,8,64,128]{4,3,2,1,0:T(8,128)(2,1)}), bf16[4,4,8,64,128]{4,3,2,1,0:T(8,128)(2,1)}, u32[]{:S(2)}, u32[]{:S(2)}) %all-to-all-start.1) | async-done | bytes 2097184 | tf_op jit(solution)/shard_map/all_to_all | solution.py:282
  157.5 4.4 all-to-all-start.2
  162.0 29.1 %dft.12 = (bf16[2,4,8,64,128]{4,3,2,1,0:T(8,128)(2,1)}, bf16[2,4,8,64,128]{4,3,2,1,0:T(8,128)(2,1)}, bf16[2,4,8,64,128]{4,3,2,1,0:T(8,128)(2,1)}, bf16[2,4,8,64,128]{4,3,2,1,0:T(8,128)(2,1)}) custom-call(s32[128,65536]{1,0:T(8,128)} %v_ref.15, f32[4,16384]{1,0:T(4,128)} %taps_ref.15, f32[2,128,128]{2,1,0:T(8,128)} %pad_maximum_fusion.flags_ref, ...), custom_call_target="tpu_custom_call" | custom-call | bytes 1024 | tf_op jit(solution)/shard_map/dft/pallas_call | solution.py:138
  193.7 3.5 join.11.rest_0_
  197.1 12.6 %all-to-all-done.2.refs_5_.refs_2_ = bf16[4,4,8,64,128]{4,3,2,1,0:T(8,128)(2,1)} async-done(((bf16[4,4,8,64,128]{4,3,2,1,0:T(8,128)(2,1)}), bf16[4,4,8,64,128]{4,3,2,1,0:T(8,128)(2,1)}, u32[]{:S(2)}, u32[]{:S(2)}) %all-to-all-start.2) | async-done | bytes 2097184 | tf_op jit(solution)/shard_map/all_to_all | solution.py:282
  209.7 3.6 all-to-all-start.3
  213.3 29.2 %dft.13 = (bf16[2,4,8,64,128]{4,3,2,1,0:T(8,128)(2,1)}, bf16[2,4,8,64,128]{4,3,2,1,0:T(8,128)(2,1)}, bf16[2,4,8,64,128]{4,3,2,1,0:T(8,128)(2,1)}, bf16[2,4,8,64,128]{4,3,2,1,0:T(8,128)(2,1)}) custom-call(s32[128,65536]{1,0:T(8,128)} %v_ref.15, f32[4,16384]{1,0:T(4,128)} %taps_ref.15, f32[2,128,128]{2,1,0:T(8,128)} %pad_maximum_fusion.flags_ref, ...), custom_call_target="tpu_custom_call" | custom-call | bytes 1024 | tf_op jit(solution)/shard_map/dft/pallas_call | solution.py:138
  248.5 12.5 %all-to-all-done.3.refs_5_.refs_3_ = bf16[4,4,8,64,128]{4,3,2,1,0:T(8,128)(2,1)S(1)} async-done(((bf16[4,4,8,64,128]{4,3,2,1,0:T(8,128)(2,1)}), bf16[4,4,8,64,128]{4,3,2,1,0:T(8,128)(2,1)S(1)}, u32[]{:S(2)}, u32[]{:S(2)}) %all-to-all-start.3) | async-done | bytes 2097184 | tf_op jit(solution)/shard_map/all_to_all | solution.py:282
  261.0 4.6 all-to-all-start.4
  265.6 29.1 %dft.14 = (bf16[2,4,8,64,128]{4,3,2,1,0:T(8,128)(2,1)}, bf16[2,4,8,64,128]{4,3,2,1,0:T(8,128)(2,1)}, bf16[2,4,8,64,128]{4,3,2,1,0:T(8,128)(2,1)}, bf16[2,4,8,64,128]{4,3,2,1,0:T(8,128)(2,1)}) custom-call(s32[128,65536]{1,0:T(8,128)} %v_ref.15, f32[4,16384]{1,0:T(4,128)} %taps_ref.15, f32[2,128,128]{2,1,0:T(8,128)} %pad_maximum_fusion.flags_ref, ...), custom_call_target="tpu_custom_call" | custom-call | bytes 1024 | tf_op jit(solution)/shard_map/dft/pallas_call | solution.py:138
  297.3 3.5 join.13.rest_0_
  300.8 12.4 %all-to-all-done.4.refs_5_.refs_4_ = bf16[4,4,8,64,128]{4,3,2,1,0:T(8,128)(2,1)} async-done(((bf16[4,4,8,64,128]{4,3,2,1,0:T(8,128)(2,1)}), bf16[4,4,8,64,128]{4,3,2,1,0:T(8,128)(2,1)}, u32[]{:S(2)}, u32[]{:S(2)}) %all-to-all-start.4) | async-done | bytes 2097184 | tf_op jit(solution)/shard_map/all_to_all | solution.py:282
  313.2 4.4 all-to-all-start.6
  317.6 29.2 %dft.15 = (bf16[2,4,8,64,128]{4,3,2,1,0:T(8,128)(2,1)}, bf16[2,4,8,64,128]{4,3,2,1,0:T(8,128)(2,1)}, bf16[2,4,8,64,128]{4,3,2,1,0:T(8,128)(2,1)}, bf16[2,4,8,64,128]{4,3,2,1,0:T(8,128)(2,1)}) custom-call(s32[128,65536]{1,0:T(8,128)} %v_ref.15, f32[4,16384]{1,0:T(4,128)} %taps_ref.15, f32[2,128,128]{2,1,0:T(8,128)} %pad_maximum_fusion.flags_ref, ...), custom_call_target="tpu_custom_call" | custom-call | bytes 1024 | tf_op jit(solution)/shard_map/dft/pallas_call | solution.py:138
  352.9 12.5 %all-to-all-done.6.refs_5_ = bf16[4,4,8,64,128]{4,3,2,1,0:T(8,128)(2,1)} async-done(((bf16[4,4,8,64,128]{4,3,2,1,0:T(8,128)(2,1)}), bf16[4,4,8,64,128]{4,3,2,1,0:T(8,128)(2,1)}, u32[]{:S(2)}, u32[]{:S(2)}) %all-to-all-start.6) | async-done | bytes 2097184 | tf_op jit(solution)/shard_map/all_to_all | solution.py:282
  365.4 3.6 all-to-all-start.5
  369.1 4.2 collective-permute-done.25.refs_1_
  373.3 20.6 %collective-permute-done.26.refs_2_ = bf16[2,4,8,64,128]{4,3,2,1,0:T(8,128)(2,1)} collective-permute-done((bf16[2,4,8,64,128]{4,3,2,1,0:T(8,128)(2,1)}, bf16[2,4,8,64,128]{4,3,2,1,0:T(8,128)(2,1)}, u32[]{:S(2)}, u32[]{:S(2)}) %collective-permute-start.26) | collective-permute-done | bytes 1048608 | tf_op jit(solution)/shard_map/ppermute | solution.py:278
  397.3 19.3 %all-to-all-done.5.refs_0_ = bf16[4,4,8,64,128]{4,3,2,1,0:T(8,128)(2,1)S(1)} async-done(((bf16[4,4,8,64,128]{4,3,2,1,0:T(8,128)(2,1)}), bf16[4,4,8,64,128]{4,3,2,1,0:T(8,128)(2,1)S(1)}, u32[]{:S(2)}, u32[]{:S(2)}) %all-to-all-start.5) | async-done | bytes 2097184 | tf_op jit(solution)/shard_map/all_to_all | solution.py:282
  417.9 3.6 all-to-all-start.7
  421.7 39.2 %correlate.2.refs_1_.refs_4_ = f32[2,8,4,128,1024]{4,3,2,1,0:T(8,128)} custom-call(s32[1]{0:T(128)} %bitcast.place, bf16[4,4,8,64,128]{4,3,2,1,0:T(8,128)(2,1)} %copy-done.3, bf16[4,4,8,64,128]{4,3,2,1,0:T(8,128)(2,1)} %all-to-all-done.1.refs_5_.refs_1_, bf16[4,4,8,64,128]{4,3,2,1,0:T(8,128)(2,1)} %all-to-all-done.2.refs_5_.refs_2_, ...), custom_call_target="tpu_custom_call" | custom-call | flops 25769803776 | bytes 33554432 | tf_op jit(solution)/shard_map/correlate/pallas_call | solution.py:245
  460.9 8.3 %all-to-all-done.7.refs_0_ = bf16[4,4,8,64,128]{4,3,2,1,0:T(8,128)(2,1)S(1)} async-done(((bf16[4,4,8,64,128]{4,3,2,1,0:T(8,128)(2,1)}), bf16[4,4,8,64,128]{4,3,2,1,0:T(8,128)(2,1)S(1)}, u32[]{:S(2)}, u32[]{:S(2)}) %all-to-all-start.7) | async-done | bytes 2097184 | tf_op jit(solution)/shard_map/all_to_all | solution.py:282
  470.6 4.4 collective-permute-done.31.refs_3_
  476.3 28.8 %correlate.3 = f32[2,8,4,128,1024]{4,3,2,1,0:T(8,128)} custom-call(s32[1]{0:T(128)} %bitcast.place, bf16[4,4,8,64,128]{4,3,2,1,0:T(8,128)(2,1)} %copy-done.1, bf16[4,4,8,64,128]{4,3,2,1,0:T(8,128)(2,1)} %after.1.refs_1_, bf16[4,4,8,64,128]{4,3,2,1,0:T(8,128)(2,1)} %collective-permute-done.30.refs_2_, ...), custom_call_target="tpu_custom_call", output_to_operand_aliasing={{}: (5, {})} | custom-call | flops 8589934592 | bytes 67108864 | tf_op jit(solution)/shard_map/correlate/pallas_call | solution.py:245
  (111 shorter events, 54.1 us)
Async XLA Ops:
  44.8 56.6 %collective-permute-start.6 = (bf16[1,4,8,64,128]{4,3,2,1,0:T(8,128)(2,1)}, bf16[1,4,8,64,128]{4,3,2,1,0:T(8,128)(2,1)}, u32[]{:S(2)}, u32[]{:S(2)}) collective-permute-start(bf16[1,4,8,64,128]{4,3,2,1,0:T(8,128)(2,1)} %get-tuple-element.46), channel_id=1, source_target_pairs={{0,6},{2,0},{4,2},{6,4},{1,7},{3,1},{5,3},{7,5},{8,14},{10,8},{12,... | collective-permute-start | bytes 1572872 | tf_op jit(solution)/shard_map/ppermute | solution.py:278
  47.1 54.4 %collective-permute-start.7 = (bf16[1,4,8,64,128]{4,3,2,1,0:T(8,128)(2,1)}, bf16[1,4,8,64,128]{4,3,2,1,0:T(8,128)(2,1)}, u32[]{:S(2)}, u32[]{:S(2)}) collective-permute-start(bf16[1,4,8,64,128]{4,3,2,1,0:T(8,128)(2,1)} %get-tuple-element.47), channel_id=1, source_target_pairs={{0,4},{2,6},{4,0},{6,2},{1,5},{3,7},{5,1},{7,3},{8,12},{10,14},{12... | collective-permute-start | bytes 1572872 | tf_op jit(solution)/shard_map/ppermute | solution.py:278
  48.7 52.9 %collective-permute-start.8 = (bf16[1,4,8,64,128]{4,3,2,1,0:T(8,128)(2,1)}, bf16[1,4,8,64,128]{4,3,2,1,0:T(8,128)(2,1)}, u32[]{:S(2)}, u32[]{:S(2)}) collective-permute-start(bf16[1,4,8,64,128]{4,3,2,1,0:T(8,128)(2,1)} %get-tuple-element.48), channel_id=1, source_target_pairs={{0,2},{2,4},{4,6},{6,0},{1,3},{3,5},{5,7},{7,1},{8,10},{10,12},{12... | collective-permute-start | bytes 1572872 | tf_op jit(solution)/shard_map/ppermute | solution.py:278
  55.4 50.0 %all-to-all-start = ((bf16[4,4,8,64,128]{4,3,2,1,0:T(8,128)(2,1)}), bf16[4,4,8,64,128]{4,3,2,1,0:T(8,128)(2,1)S(1)}, u32[]{:S(2)}, u32[]{:S(2)}) async-start(bf16[4,4,8,64,128]{4,3,2,1,0:T(8,128)(2,1)} %join.8.rest_0_), calls=%async_computation | async-start | bytes 4194304 | tf_op jit(solution)/shard_map/all_to_all | solution.py:282
  90.4 52.5 %collective-permute-start.3 = (bf16[2,4,8,64,128]{4,3,2,1,0:T(8,128)(2,1)}, bf16[2,4,8,64,128]{4,3,2,1,0:T(8,128)(2,1)S(1)}, u32[]{:S(2)}, u32[]{:S(2)}) collective-permute-start(bf16[2,4,8,64,128]{4,3,2,1,0:T(8,128)(2,1)} %get-tuple-element.43), channel_id=1, source_target_pairs={{0,6},{2,0},{4,2},{6,4},{1,7},{3,1},{5,3},{7,5},{8,14},{10,8},{12,... | collective-permute-start | bytes 3145736 | tf_op jit(solution)/shard_map/ppermute | solution.py:278
  105.3 52.2 %all-to-all-start.1 = ((bf16[4,4,8,64,128]{4,3,2,1,0:T(8,128)(2,1)}), bf16[4,4,8,64,128]{4,3,2,1,0:T(8,128)(2,1)}, u32[]{:S(2)}, u32[]{:S(2)}) async-start(bf16[4,4,8,64,128]{4,3,2,1,0:T(8,128)(2,1)} %join.9.rest_0_), calls=%async_computation.1 | async-start | bytes 4194304 | tf_op jit(solution)/shard_map/all_to_all | solution.py:282
  139.1 52.1 %collective-permute-start.12 = (bf16[2,4,8,64,128]{4,3,2,1,0:T(8,128)(2,1)}, bf16[2,4,8,64,128]{4,3,2,1,0:T(8,128)(2,1)}, u32[]{:S(2)}, u32[]{:S(2)}) collective-permute-start(bf16[2,4,8,64,128]{4,3,2,1,0:T(8,128)(2,1)} %get-tuple-element.54), channel_id=1, source_target_pairs={{0,6},{2,0},{4,2},{6,4},{1,7},{3,1},{5,3},{7,5},{8,14},{10,8},{12,... | collective-permute-start | bytes 3145736 | tf_op jit(solution)/shard_map/ppermute | solution.py:278
  141.4 50.3 %collective-permute-start.13 = (bf16[2,4,8,64,128]{4,3,2,1,0:T(8,128)(2,1)}, bf16[2,4,8,64,128]{4,3,2,1,0:T(8,128)(2,1)}, u32[]{:S(2)}, u32[]{:S(2)}) collective-permute-start(bf16[2,4,8,64,128]{4,3,2,1,0:T(8,128)(2,1)} %get-tuple-element.55), channel_id=1, source_target_pairs={{0,4},{2,6},{4,0},{6,2},{1,5},{3,7},{5,1},{7,3},{8,12},{10,14},{12... | collective-permute-start | bytes 3145736 | tf_op jit(solution)/shard_map/ppermute | solution.py:278
  142.9 50.8 %collective-permute-start.14 = (bf16[2,4,8,64,128]{4,3,2,1,0:T(8,128)(2,1)}, bf16[2,4,8,64,128]{4,3,2,1,0:T(8,128)(2,1)}, u32[]{:S(2)}, u32[]{:S(2)}) collective-permute-start(bf16[2,4,8,64,128]{4,3,2,1,0:T(8,128)(2,1)} %get-tuple-element.56), channel_id=1, source_target_pairs={{0,2},{2,4},{4,6},{6,0},{1,3},{3,5},{5,7},{7,1},{8,10},{10,12},{12... | collective-permute-start | bytes 3145736 | tf_op jit(solution)/shard_map/ppermute | solution.py:278
  142.9 50.7 %collective-permute-start.15 = (bf16[4,4,8,64,128]{4,3,2,1,0:T(8,128)(2,1)S(1)}, bf16[4,4,8,64,128]{4,3,2,1,0:T(8,128)(2,1)}, u32[]{:S(2)}, u32[]{:S(2)}) collective-permute-start(bf16[4,4,8,64,128]{4,3,2,1,0:T(8,128)(2,1)S(1)} %all-to-all-done.refs_5_.refs_0_), channel_id=1, source_target_pairs={{0,1},{1,0},{2,3},{3,2},{4,5},{5,4},{6,7},{7,6},{8,9},{9,8},{10,11... | collective-permute-start | bytes 6291464 | tf_op jit(solution)/shard_map/ppermute | solution.py:278
  157.5 52.2 %all-to-all-start.2 = ((bf16[4,4,8,64,128]{4,3,2,1,0:T(8,128)(2,1)}), bf16[4,4,8,64,128]{4,3,2,1,0:T(8,128)(2,1)}, u32[]{:S(2)}, u32[]{:S(2)}) async-start(bf16[4,4,8,64,128]{4,3,2,1,0:T(8,128)(2,1)} %join.10.rest_0_), calls=%async_computation.2 | async-start | bytes 4194304 | tf_op jit(solution)/shard_map/all_to_all | solution.py:282
  191.1 51.4 %collective-permute-start.9 = (bf16[2,4,8,64,128]{4,3,2,1,0:T(8,128)(2,1)}, bf16[2,4,8,64,128]{4,3,2,1,0:T(8,128)(2,1)S(1)}, u32[]{:S(2)}, u32[]{:S(2)}) collective-permute-start(bf16[2,4,8,64,128]{4,3,2,1,0:T(8,128)(2,1)} %get-tuple-element.51), channel_id=1, source_target_pairs={{0,6},{2,0},{4,2},{6,4},{1,7},{3,1},{5,3},{7,5},{8,14},{10,8},{12,... | collective-permute-start | bytes 3145736 | tf_op jit(solution)/shard_map/ppermute | solution.py:278
  191.1 52.0 %collective-permute-start.10 = (bf16[2,4,8,64,128]{4,3,2,1,0:T(8,128)(2,1)}, bf16[2,4,8,64,128]{4,3,2,1,0:T(8,128)(2,1)}, u32[]{:S(2)}, u32[]{:S(2)}) collective-permute-start(bf16[2,4,8,64,128]{4,3,2,1,0:T(8,128)(2,1)} %get-tuple-element.52), channel_id=1, source_target_pairs={{0,4},{2,6},{4,0},{6,2},{1,5},{3,7},{5,1},{7,3},{8,12},{10,14},{12... | collective-permute-start | bytes 3145736 | tf_op jit(solution)/shard_map/ppermute | solution.py:278
  191.7 53.4 %collective-permute-start.11 = (bf16[2,4,8,64,128]{4,3,2,1,0:T(8,128)(2,1)}, bf16[2,4,8,64,128]{4,3,2,1,0:T(8,128)(2,1)}, u32[]{:S(2)}, u32[]{:S(2)}) collective-permute-start(bf16[2,4,8,64,128]{4,3,2,1,0:T(8,128)(2,1)} %get-tuple-element.53), channel_id=1, source_target_pairs={{0,2},{2,4},{4,6},{6,0},{1,3},{3,5},{5,7},{7,1},{8,10},{10,12},{12... | collective-permute-start | bytes 3145736 | tf_op jit(solution)/shard_map/ppermute | solution.py:278
  193.6 51.4 %collective-permute-start.16 = (bf16[4,4,8,64,128]{4,3,2,1,0:T(8,128)(2,1)}, bf16[4,4,8,64,128]{4,3,2,1,0:T(8,128)(2,1)}, u32[]{:S(2)}, u32[]{:S(2)}) collective-permute-start(bf16[4,4,8,64,128]{4,3,2,1,0:T(8,128)(2,1)} %all-to-all-done.1.refs_5_.refs_1_), channel_id=1, source_target_pairs={{0,1},{1,0},{2,3},{3,2},{4,5},{5,4},{6,7},{7,6},{8,9},{9,8},{10,11... | collective-permute-start | bytes 6291464 | tf_op jit(solution)/shard_map/ppermute | solution.py:278
  209.7 51.3 %all-to-all-start.3 = ((bf16[4,4,8,64,128]{4,3,2,1,0:T(8,128)(2,1)}), bf16[4,4,8,64,128]{4,3,2,1,0:T(8,128)(2,1)S(1)}, u32[]{:S(2)}, u32[]{:S(2)}) async-start(bf16[4,4,8,64,128]{4,3,2,1,0:T(8,128)(2,1)} %join.11.rest_0_), calls=%async_computation.3 | async-start | bytes 4194304 | tf_op jit(solution)/shard_map/all_to_all | solution.py:282
  242.5 52.3 %collective-permute-start.20 = (bf16[2,4,8,64,128]{4,3,2,1,0:T(8,128)(2,1)}, bf16[2,4,8,64,128]{4,3,2,1,0:T(8,128)(2,1)}, u32[]{:S(2)}, u32[]{:S(2)}) collective-permute-start(bf16[2,4,8,64,128]{4,3,2,1,0:T(8,128)(2,1)} %get-tuple-element.62), channel_id=1, source_target_pairs={{0,6},{2,0},{4,2},{6,4},{1,7},{3,1},{5,3},{7,5},{8,14},{10,8},{12,... | collective-permute-start | bytes 3145736 | tf_op jit(solution)/shard_map/ppermute | solution.py:278
  242.5 52.8 %collective-permute-start.21 = (bf16[2,4,8,64,128]{4,3,2,1,0:T(8,128)(2,1)}, bf16[2,4,8,64,128]{4,3,2,1,0:T(8,128)(2,1)}, u32[]{:S(2)}, u32[]{:S(2)}) collective-permute-start(bf16[2,4,8,64,128]{4,3,2,1,0:T(8,128)(2,1)} %get-tuple-element.63), channel_id=1, source_target_pairs={{0,4},{2,6},{4,0},{6,2},{1,5},{3,7},{5,1},{7,3},{8,12},{10,14},{12... | collective-permute-start | bytes 3145736 | tf_op jit(solution)/shard_map/ppermute | solution.py:278
  243.1 54.2 %collective-permute-start.22 = (bf16[2,4,8,64,128]{4,3,2,1,0:T(8,128)(2,1)}, bf16[2,4,8,64,128]{4,3,2,1,0:T(8,128)(2,1)}, u32[]{:S(2)}, u32[]{:S(2)}) collective-permute-start(bf16[2,4,8,64,128]{4,3,2,1,0:T(8,128)(2,1)} %get-tuple-element.64), channel_id=1, source_target_pairs={{0,2},{2,4},{4,6},{6,0},{1,3},{3,5},{5,7},{7,1},{8,10},{10,12},{12... | collective-permute-start | bytes 3145736 | tf_op jit(solution)/shard_map/ppermute | solution.py:278
  245.0 52.3 %collective-permute-start.23 = (bf16[4,4,8,64,128]{4,3,2,1,0:T(8,128)(2,1)}, bf16[4,4,8,64,128]{4,3,2,1,0:T(8,128)(2,1)}, u32[]{:S(2)}, u32[]{:S(2)}) collective-permute-start(bf16[4,4,8,64,128]{4,3,2,1,0:T(8,128)(2,1)} %all-to-all-done.2.refs_5_.refs_2_), channel_id=1, source_target_pairs={{0,1},{1,0},{2,3},{3,2},{4,5},{5,4},{6,7},{7,6},{8,9},{9,8},{10,11... | collective-permute-start | bytes 6291464 | tf_op jit(solution)/shard_map/ppermute | solution.py:278
  261.0 52.2 %all-to-all-start.4 = ((bf16[4,4,8,64,128]{4,3,2,1,0:T(8,128)(2,1)}), bf16[4,4,8,64,128]{4,3,2,1,0:T(8,128)(2,1)}, u32[]{:S(2)}, u32[]{:S(2)}) async-start(bf16[4,4,8,64,128]{4,3,2,1,0:T(8,128)(2,1)} %join.12.rest_0_), calls=%async_computation.4 | async-start | bytes 4194304 | tf_op jit(solution)/shard_map/all_to_all | solution.py:282
  294.7 52.2 %collective-permute-start.17 = (bf16[2,4,8,64,128]{4,3,2,1,0:T(8,128)(2,1)}, bf16[2,4,8,64,128]{4,3,2,1,0:T(8,128)(2,1)S(1)}, u32[]{:S(2)}, u32[]{:S(2)}) collective-permute-start(bf16[2,4,8,64,128]{4,3,2,1,0:T(8,128)(2,1)} %get-tuple-element.59), channel_id=1, source_target_pairs={{0,6},{2,0},{4,2},{6,4},{1,7},{3,1},{5,3},{7,5},{8,14},{10,8},{12,... | collective-permute-start | bytes 3145736 | tf_op jit(solution)/shard_map/ppermute | solution.py:278
  294.8 52.7 %collective-permute-start.18 = (bf16[2,4,8,64,128]{4,3,2,1,0:T(8,128)(2,1)}, bf16[2,4,8,64,128]{4,3,2,1,0:T(8,128)(2,1)}, u32[]{:S(2)}, u32[]{:S(2)}) collective-permute-start(bf16[2,4,8,64,128]{4,3,2,1,0:T(8,128)(2,1)} %get-tuple-element.60), channel_id=1, source_target_pairs={{0,4},{2,6},{4,0},{6,2},{1,5},{3,7},{5,1},{7,3},{8,12},{10,14},{12... | collective-permute-start | bytes 3145736 | tf_op jit(solution)/shard_map/ppermute | solution.py:278
  295.3 54.1 %collective-permute-start.19 = (bf16[2,4,8,64,128]{4,3,2,1,0:T(8,128)(2,1)}, bf16[2,4,8,64,128]{4,3,2,1,0:T(8,128)(2,1)}, u32[]{:S(2)}, u32[]{:S(2)}) collective-permute-start(bf16[2,4,8,64,128]{4,3,2,1,0:T(8,128)(2,1)} %get-tuple-element.61), channel_id=1, source_target_pairs={{0,2},{2,4},{4,6},{6,0},{1,3},{3,5},{5,7},{7,1},{8,10},{10,12},{12... | collective-permute-start | bytes 3145736 | tf_op jit(solution)/shard_map/ppermute | solution.py:278
  297.3 52.1 %collective-permute-start.24 = (bf16[4,4,8,64,128]{4,3,2,1,0:T(8,128)(2,1)S(1)}, bf16[4,4,8,64,128]{4,3,2,1,0:T(8,128)(2,1)}, u32[]{:S(2)}, u32[]{:S(2)}) collective-permute-start(bf16[4,4,8,64,128]{4,3,2,1,0:T(8,128)(2,1)S(1)} %all-to-all-done.3.refs_5_.refs_3_), channel_id=1, source_target_pairs={{0,1},{1,0},{2,3},{3,2},{4,5},{5,4},{6,7},{7,6},{8,9},{9,8},{10,11... | collective-permute-start | bytes 6291464 | tf_op jit(solution)/shard_map/ppermute | solution.py:278
  313.2 52.2 %all-to-all-start.6 = ((bf16[4,4,8,64,128]{4,3,2,1,0:T(8,128)(2,1)}), bf16[4,4,8,64,128]{4,3,2,1,0:T(8,128)(2,1)}, u32[]{:S(2)}, u32[]{:S(2)}) async-start(bf16[4,4,8,64,128]{4,3,2,1,0:T(8,128)(2,1)} %join.13.rest_0_), calls=%async_computation.6 | async-start | bytes 4194304 | tf_op jit(solution)/shard_map/all_to_all | solution.py:282
  346.9 47.0 %collective-permute-start.26 = (bf16[2,4,8,64,128]{4,3,2,1,0:T(8,128)(2,1)}, bf16[2,4,8,64,128]{4,3,2,1,0:T(8,128)(2,1)}, u32[]{:S(2)}, u32[]{:S(2)}) collective-permute-start(bf16[2,4,8,64,128]{4,3,2,1,0:T(8,128)(2,1)} %get-tuple-element.67), channel_id=1, source_target_pairs={{0,4},{2,6},{4,0},{6,2},{1,5},{3,7},{5,1},{7,3},{8,12},{10,14},{12... | collective-permute-start | bytes 3145736 | tf_op jit(solution)/shard_map/ppermute | solution.py:278
  347.5 46.4 %collective-permute-start.27 = (bf16[2,4,8,64,128]{4,3,2,1,0:T(8,128)(2,1)}, bf16[2,4,8,64,128]{4,3,2,1,0:T(8,128)(2,1)}, u32[]{:S(2)}, u32[]{:S(2)}) collective-permute-start(bf16[2,4,8,64,128]{4,3,2,1,0:T(8,128)(2,1)} %get-tuple-element.68), channel_id=1, source_target_pairs={{0,2},{2,4},{4,6},{6,0},{1,3},{3,5},{5,7},{7,1},{8,10},{10,12},{12... | collective-permute-start | bytes 3145736 | tf_op jit(solution)/shard_map/ppermute | solution.py:278
  365.4 51.3 %all-to-all-start.5 = ((bf16[4,4,8,64,128]{4,3,2,1,0:T(8,128)(2,1)}), bf16[4,4,8,64,128]{4,3,2,1,0:T(8,128)(2,1)S(1)}, u32[]{:S(2)}, u32[]{:S(2)}) async-start(bf16[4,4,8,64,128]{4,3,2,1,0:T(8,128)(2,1)} %join.14.refs_4_), calls=%async_computation.5 | async-start | bytes 4194304 | tf_op jit(solution)/shard_map/all_to_all | solution.py:282
  369.0 52.7 %collective-permute-start.29 = (bf16[4,4,8,64,128]{4,3,2,1,0:T(8,128)(2,1)}, bf16[4,4,8,64,128]{4,3,2,1,0:T(8,128)(2,1)}, u32[]{:S(2)}, u32[]{:S(2)}) collective-permute-start(bf16[4,4,8,64,128]{4,3,2,1,0:T(8,128)(2,1)} %all-to-all-done.6.refs_5_), channel_id=1, source_target_pairs={{0,1},{1,0},{2,3},{3,2},{4,5},{5,4},{6,7},{7,6},{8,9},{9,8},{10,11... | collective-permute-start | bytes 6291464 | tf_op jit(solution)/shard_map/ppermute | solution.py:278
  417.9 51.3 %all-to-all-start.7 = ((bf16[4,4,8,64,128]{4,3,2,1,0:T(8,128)(2,1)}), bf16[4,4,8,64,128]{4,3,2,1,0:T(8,128)(2,1)S(1)}, u32[]{:S(2)}, u32[]{:S(2)}) async-start(bf16[4,4,8,64,128]{4,3,2,1,0:T(8,128)(2,1)} %join.15), calls=%async_computation.7 | async-start | bytes 4194304 | tf_op jit(solution)/shard_map/all_to_all | solution.py:282
  421.6 49.0 %collective-permute-start.30 = (bf16[4,4,8,64,128]{4,3,2,1,0:T(8,128)(2,1)}, bf16[4,4,8,64,128]{4,3,2,1,0:T(8,128)(2,1)}, u32[]{:S(2)}, u32[]{:S(2)}) collective-permute-start(bf16[4,4,8,64,128]{4,3,2,1,0:T(8,128)(2,1)} %copy-done.1), channel_id=1, source_target_pairs={{0,1},{1,0},{2,3},{3,2},{4,5},{5,4},{6,7},{7,6},{8,9},{9,8},{10,11... | collective-permute-start | bytes 6291464 | tf_op jit(solution)/shard_map/ppermute | solution.py:278
  (21 other events, 335.8 us)

commit v3 on v2

--- a/solution.py
+++ b/solution.py
@@ -56,7 +56,7 @@
     return table_one, twists, table_two
 
 
-def dft_kernel(items, length, deps, v_ref, taps_ref, flags_ref, one_ref, twist_ref, two_ref, *rest):
+def dft_kernel(items, length, deps, place, v_ref, taps_ref, flags_ref, one_ref, twist_ref, two_ref, *rest):
     outs = rest[deps:-2]
     samples, results = rest[-2:]
     rows = v_ref.shape[0]
@@ -83,7 +83,7 @@
     lower = lax.broadcasted_iota(jnp.int32, (LANES // 2, LANES), 1) < LANES // 2
     half = LANES // 2
 
-    @pl.loop(0, len(items) * rows // 2, unroll=4)
+    @pl.loop(0, len(items) * rows // 2, unroll=8)
     def _(pair):
         base = pl.multiple_of(pair * 2 * PAD, 8)
         data = jnp.concatenate(
@@ -119,13 +119,14 @@
             results[pl.ds(start + rows, half, stride=2 * rows), :] = odd
 
     share = LANES * rows // len(outs)
-    for to, out in enumerate(outs):
+    for step, out in enumerate(outs):
+        home = lax.rem(place[1] + step, len(outs))
         for index in range(len(items)):
-            chunk = results[pl.ds(index * LANES * rows + to * share, share), :]
-            out[index] = chunk.astype(BF16).reshape(out.shape[1:])
-
-
-def dft(items, voltages, taps, flags, one, twist, two, peers, blocks, part, parts, deps=()):
+            start = pl.multiple_of(index * LANES * rows + home * share, share)
+            out[index] = results[pl.ds(start, share), :].astype(BF16).reshape(out.shape[1:])
+
+
+def dft(items, place, voltages, taps, flags, one, twist, two, peers, blocks, part, parts, deps=()):
     inputs = voltages.shape[0] // parts
     length = taps.shape[1]
     rows = 16
@@ -139,6 +140,7 @@
         functools.partial(dft_kernel, items, length, len(deps)),
         grid=(steps,),
         in_specs=[
+            pl.BlockSpec(memory_space=pltpu.SMEM),
             pl.BlockSpec((rows, voltages.shape[1]), lambda i: (i + part * steps, 0)),
             whole(taps.shape),
             pl.BlockSpec((count, rows, LANES), lambda i: (0, i + part * steps, 0)),
@@ -156,7 +158,7 @@
         compiler_params=pltpu.CompilerParams(vmem_limit_bytes=VMEM_LIMIT),
         cost_estimate=pl.CostEstimate(flops=0, bytes_accessed=1024, transcendentals=0),
         name="dft",
-    )(voltages, taps, flags, one, twist, two, *deps)
+    )(place, voltages, taps, flags, one, twist, two, *deps)
 
 
 def join_kernel(peers, partial, *refs):
@@ -290,14 +292,11 @@
     blocks, peers = lax.axis_size("inp"), lax.axis_size("tm")
     t, core = lax.axis_index("tm"), lax.axis_index("bl")
     table_one, twists, table_two = tables(length)
-    place = jnp.stack([core]).astype(jnp.int32)
+    place = jnp.stack([core, t]).astype(jnp.int32)
 
     per = LANES // 2 // (blocks * peers)
-    home_t = (t + jnp.arange(peers, dtype=jnp.int32)) % peers
-    home_z = jnp.arange(blocks, dtype=jnp.int32)
-    order = (home_z[None, :] * peers + home_t[:, None])[:, :, None] * per
-    order = (order + jnp.arange(per, dtype=jnp.int32)).reshape(-1)
-    two = jnp.take(jnp.asarray(table_two), order, axis=2).reshape(2 * LANES, 2 * LANES)
+    order = np.arange(LANES // 2).reshape(blocks, peers, per).transpose(1, 0, 2).reshape(-1)
+    two = jnp.asarray(table_two[:, :, order].reshape(2 * LANES, 2 * LANES))
     one, twist = jnp.asarray(table_one), jnp.asarray(twists)
 
     keep = jnp.broadcast_to(flags.astype(F32)[:, None], (flags.shape[0], LANES))
@@ -316,7 +315,7 @@
         if partial(c):
             items.append([(k, j + k - spectra) for k in range(reach) if j + k >= spectra])
         sent = dft(
-            items, voltages, taps, keep_two[: len(items)], one, twist, two, peers, blocks,
+            items, place, voltages, taps, keep_two[: len(items)], one, twist, two, peers, blocks,
             part, parts, last,
         )
         last[:] = [sent[0]]

time: 506 us -> 502 us (level)
  Pallas kernels: 305 us -> 286 us
  waiting for transfers between devices: 121 us -> 139 us
    pallas_call x8, Pallas kernels: 211 us -> 192 us  [dft(): pl.pallas_call(functools.partial(dft_kernel, items, length, len(deps)), g...]
    all_to_all x8, waiting for transfers between devices: 89 us -> 107 us  [turn(): return lax.all_to_all(value, axis, split_axis=0, concat_axis=0, tiled=True)]
  transfers between devices with their start and end apart: 40 -> 40, of which waited for: 12 -> 12; matrix products, arithmetic and copies ran while one was open for 0% -> 0% of each run, Pallas kernels for 51% -> 48%
where the time goes in v3:
time: 502 us; the launch traced here: 501 us
  Pallas kernels  286 us (57%)
  waiting for transfers between devices  139 us (28%)
  starting transfers between devices  67.3 us (13%)
  local copies, waits for them, and re-layouts  6.66 us (1%)
    pallas_call x8, Pallas kernels, dft(): pl.pallas_call(functools.partial(dft_kernel, items, length, len(deps)), g...  192 us
    all_to_all x8, waiting for transfers between devices, turn(): return lax.all_to_all(value, axis, split_axis=0, concat_axis=0, tiled=True)  107 us
    pallas_call x2, Pallas kernels, correlate(): pl.pallas_call(functools.partial(correlate_kernel, stages, parts, scale,...  68.2 us
    all_to_all x8, starting transfers between devices, turn(): return lax.all_to_all(value, axis, split_axis=0, concat_axis=0, tiled=True)  34 us
    ppermute x32, starting transfers between devices, shift(): lax.ppermute(value, axis, [(i, (i + step) % count) for i in range(count)])  33.3 us
    ppermute x32, waiting for transfers between devices, shift(): lax.ppermute(value, axis, [(i, (i + step) % count) for i in range(count)])  31.9 us
    pallas_call x8, Pallas kernels, join(): pl.pallas_call(functools.partial(join_kernel, peers, partial), grid=(inpu...  26 us
  transfers between devices with their start and end apart: 40, of which 12 were waited for; matrix products, arithmetic and copies ran while one was open for 0% of the time, Pallas kernels for 48%

profile of v3, /device:TPU:0, one launch (start us, length us, event | category | flops | bytes accessed | tf_op | source)
XLA Modules:
  0.0 500.8 jit_solution(4707176422832028176)
XLA Ops:
  2.0 15.7 %dft.8 = (bf16[1,4,8,64,128]{4,3,2,1,0:T(8,128)(2,1)}, bf16[1,4,8,64,128]{4,3,2,1,0:T(8,128)(2,1)}, bf16[1,4,8,64,128]{4,3,2,1,0:T(8,128)(2,1)}, bf16[1,4,8,64,128]{4,3,2,1,0:T(8,128)(2,1)}) custom-call(s32[2]{0:T(128)} %pad_add_fusion.place, s32[128,65536]{1,0:T(8,128)} %v_ref.15, f32[4,16384]{1,0:T(4,128)} %taps_ref.15, ...), custom_call_target="tpu_custom_call" | custom-call | bytes 1024 | tf_op jit(solution)/shard_map/dft/pallas_call | solution.py:139
  17.7 3.9 collective-permute-start
  22.7 15.8 %dft.9 = (bf16[1,4,8,64,128]{4,3,2,1,0:T(8,128)(2,1)}, bf16[1,4,8,64,128]{4,3,2,1,0:T(8,128)(2,1)}, bf16[1,4,8,64,128]{4,3,2,1,0:T(8,128)(2,1)}, bf16[1,4,8,64,128]{4,3,2,1,0:T(8,128)(2,1)}) custom-call(s32[2]{0:T(128)} %pad_add_fusion.place, s32[128,65536]{1,0:T(8,128)} %v_ref.15, f32[4,16384]{1,0:T(4,128)} %taps_ref.15, ...), custom_call_target="tpu_custom_call" | custom-call | bytes 1024 | tf_op jit(solution)/shard_map/dft/pallas_call | solution.py:139
  42.4 5.1 %collective-permute-done.1.refs_2_ = bf16[1,4,8,64,128]{4,3,2,1,0:T(8,128)(2,1)S(1)} collective-permute-done((bf16[1,4,8,64,128]{4,3,2,1,0:T(8,128)(2,1)}, bf16[1,4,8,64,128]{4,3,2,1,0:T(8,128)(2,1)S(1)}, u32[]{:S(2)}, u32[]{:S(2)}) %collective-permute-start.1) | collective-permute-done | bytes 524320 | tf_op jit(solution)/shard_map/ppermute | solution.py:280
  51.1 5.0 all-to-all-start
  56.9 26.8 %dft.10 = (bf16[2,4,8,64,128]{4,3,2,1,0:T(8,128)(2,1)}, bf16[2,4,8,64,128]{4,3,2,1,0:T(8,128)(2,1)}, bf16[2,4,8,64,128]{4,3,2,1,0:T(8,128)(2,1)}, bf16[2,4,8,64,128]{4,3,2,1,0:T(8,128)(2,1)}) custom-call(s32[2]{0:T(128)} %pad_add_fusion.place, s32[128,65536]{1,0:T(8,128)} %v_ref.15, f32[4,16384]{1,0:T(4,128)} %taps_ref.15, ...), custom_call_target="tpu_custom_call" | custom-call | bytes 1024 | tf_op jit(solution)/shard_map/dft/pallas_call | solution.py:139
  83.6 10.4 %collective-permute-start.3 = (bf16[2,4,8,64,128]{4,3,2,1,0:T(8,128)(2,1)}, bf16[2,4,8,64,128]{4,3,2,1,0:T(8,128)(2,1)S(1)}, u32[]{:S(2)}, u32[]{:S(2)}) collective-permute-start(bf16[2,4,8,64,128]{4,3,2,1,0:T(8,128)(2,1)} %get-tuple-element.43), channel_id=1, source_target_pairs={{0,6},{2,0},{4,2},{6,4},{1,7},{3,1},{5,3},{7,5},{8,14},{10,8},{12,... | collective-permute-start | bytes 3145736 | tf_op jit(solution)/shard_map/ppermute | solution.py:280
  97.4 3.6 all-to-all-done.refs_5_.refs_0_
  101.0 4.5 all-to-all-start.1
  105.5 26.8 %dft.11 = (bf16[2,4,8,64,128]{4,3,2,1,0:T(8,128)(2,1)}, bf16[2,4,8,64,128]{4,3,2,1,0:T(8,128)(2,1)}, bf16[2,4,8,64,128]{4,3,2,1,0:T(8,128)(2,1)}, bf16[2,4,8,64,128]{4,3,2,1,0:T(8,128)(2,1)}) custom-call(s32[2]{0:T(128)} %pad_add_fusion.place, s32[128,65536]{1,0:T(8,128)} %v_ref.15, f32[4,16384]{1,0:T(4,128)} %taps_ref.15, ...), custom_call_target="tpu_custom_call" | custom-call | bytes 1024 | tf_op jit(solution)/shard_map/dft/pallas_call | solution.py:139
  139.7 13.6 %all-to-all-done.1.refs_5_.refs_1_ = bf16[4,4,8,64,128]{4,3,2,1,0:T(8,128)(2,1)} async-done(((bf16[4,4,8,64,128]{4,3,2,1,0:T(8,128)(2,1)}), bf16[4,4,8,64,128]{4,3,2,1,0:T(8,128)(2,1)}, u32[]{:S(2)}, u32[]{:S(2)}) %all-to-all-start.1) | async-done | bytes 2097184 | tf_op jit(solution)/shard_map/all_to_all | solution.py:284
  153.2 4.6 all-to-all-start.2
  157.8 26.6 %dft.12 = (bf16[2,4,8,64,128]{4,3,2,1,0:T(8,128)(2,1)}, bf16[2,4,8,64,128]{4,3,2,1,0:T(8,128)(2,1)}, bf16[2,4,8,64,128]{4,3,2,1,0:T(8,128)(2,1)}, bf16[2,4,8,64,128]{4,3,2,1,0:T(8,128)(2,1)}) custom-call(s32[2]{0:T(128)} %pad_add_fusion.place, s32[128,65536]{1,0:T(8,128)} %v_ref.15, f32[4,16384]{1,0:T(4,128)} %taps_ref.15, ...), custom_call_target="tpu_custom_call" | custom-call | bytes 1024 | tf_op jit(solution)/shard_map/dft/pallas_call | solution.py:139
  190.5 14.9 %all-to-all-done.2.refs_5_.refs_2_ = bf16[4,4,8,64,128]{4,3,2,1,0:T(8,128)(2,1)} async-done(((bf16[4,4,8,64,128]{4,3,2,1,0:T(8,128)(2,1)}), bf16[4,4,8,64,128]{4,3,2,1,0:T(8,128)(2,1)}, u32[]{:S(2)}, u32[]{:S(2)}) %all-to-all-start.2) | async-done | bytes 2097184 | tf_op jit(solution)/shard_map/all_to_all | solution.py:284
  205.4 3.6 all-to-all-start.3
  209.0 26.7 %dft.13 = (bf16[2,4,8,64,128]{4,3,2,1,0:T(8,128)(2,1)}, bf16[2,4,8,64,128]{4,3,2,1,0:T(8,128)(2,1)}, bf16[2,4,8,64,128]{4,3,2,1,0:T(8,128)(2,1)}, bf16[2,4,8,64,128]{4,3,2,1,0:T(8,128)(2,1)}) custom-call(s32[2]{0:T(128)} %pad_add_fusion.place, s32[128,65536]{1,0:T(8,128)} %v_ref.15, f32[4,16384]{1,0:T(4,128)} %taps_ref.15, ...), custom_call_target="tpu_custom_call" | custom-call | bytes 1024 | tf_op jit(solution)/shard_map/dft/pallas_call | solution.py:139
  241.7 15.0 %all-to-all-done.3.refs_5_.refs_3_ = bf16[4,4,8,64,128]{4,3,2,1,0:T(8,128)(2,1)S(1)} async-done(((bf16[4,4,8,64,128]{4,3,2,1,0:T(8,128)(2,1)}), bf16[4,4,8,64,128]{4,3,2,1,0:T(8,128)(2,1)S(1)}, u32[]{:S(2)}, u32[]{:S(2)}) %all-to-all-start.3) | async-done | bytes 2097184 | tf_op jit(solution)/shard_map/all_to_all | solution.py:284
  256.7 4.4 all-to-all-start.4
  261.1 26.7 %dft.14 = (bf16[2,4,8,64,128]{4,3,2,1,0:T(8,128)(2,1)}, bf16[2,4,8,64,128]{4,3,2,1,0:T(8,128)(2,1)}, bf16[2,4,8,64,128]{4,3,2,1,0:T(8,128)(2,1)}, bf16[2,4,8,64,128]{4,3,2,1,0:T(8,128)(2,1)}) custom-call(s32[2]{0:T(128)} %pad_add_fusion.place, s32[128,65536]{1,0:T(8,128)} %v_ref.15, f32[4,16384]{1,0:T(4,128)} %taps_ref.15, ...), custom_call_target="tpu_custom_call" | custom-call | bytes 1024 | tf_op jit(solution)/shard_map/dft/pallas_call | solution.py:139
  290.4 3.5 join.13.rest_0_
  293.9 15.0 %all-to-all-done.4.refs_5_.refs_4_ = bf16[4,4,8,64,128]{4,3,2,1,0:T(8,128)(2,1)} async-done(((bf16[4,4,8,64,128]{4,3,2,1,0:T(8,128)(2,1)}), bf16[4,4,8,64,128]{4,3,2,1,0:T(8,128)(2,1)}, u32[]{:S(2)}, u32[]{:S(2)}) %all-to-all-start.4) | async-done | bytes 2097184 | tf_op jit(solution)/shard_map/all_to_all | solution.py:284
  308.9 4.4 all-to-all-start.6
  313.3 26.7 %dft.15 = (bf16[2,4,8,64,128]{4,3,2,1,0:T(8,128)(2,1)}, bf16[2,4,8,64,128]{4,3,2,1,0:T(8,128)(2,1)}, bf16[2,4,8,64,128]{4,3,2,1,0:T(8,128)(2,1)}, bf16[2,4,8,64,128]{4,3,2,1,0:T(8,128)(2,1)}) custom-call(s32[2]{0:T(128)} %pad_add_fusion.place, s32[128,65536]{1,0:T(8,128)} %v_ref.15, f32[4,16384]{1,0:T(4,128)} %taps_ref.15, ...), custom_call_target="tpu_custom_call" | custom-call | bytes 1024 | tf_op jit(solution)/shard_map/dft/pallas_call | solution.py:139
  346.0 15.0 %all-to-all-done.6.refs_5_ = bf16[4,4,8,64,128]{4,3,2,1,0:T(8,128)(2,1)} async-done(((bf16[4,4,8,64,128]{4,3,2,1,0:T(8,128)(2,1)}), bf16[4,4,8,64,128]{4,3,2,1,0:T(8,128)(2,1)}, u32[]{:S(2)}, u32[]{:S(2)}) %all-to-all-start.6) | async-done | bytes 2097184 | tf_op jit(solution)/shard_map/all_to_all | solution.py:284
  361.1 3.6 all-to-all-start.5
  366.5 20.6 %collective-permute-done.26.refs_2_ = bf16[2,4,8,64,128]{4,3,2,1,0:T(8,128)(2,1)} collective-permute-done((bf16[2,4,8,64,128]{4,3,2,1,0:T(8,128)(2,1)}, bf16[2,4,8,64,128]{4,3,2,1,0:T(8,128)(2,1)}, u32[]{:S(2)}, u32[]{:S(2)}) %collective-permute-start.26) | collective-permute-done | bytes 1048608 | tf_op jit(solution)/shard_map/ppermute | solution.py:280
  390.5 21.8 %all-to-all-done.5.refs_0_ = bf16[4,4,8,64,128]{4,3,2,1,0:T(8,128)(2,1)S(1)} async-done(((bf16[4,4,8,64,128]{4,3,2,1,0:T(8,128)(2,1)}), bf16[4,4,8,64,128]{4,3,2,1,0:T(8,128)(2,1)S(1)}, u32[]{:S(2)}, u32[]{:S(2)}) %all-to-all-start.5) | async-done | bytes 2097184 | tf_op jit(solution)/shard_map/all_to_all | solution.py:284
  413.6 3.8 all-to-all-start.7
  417.6 39.3 %correlate.2.refs_1_.refs_4_ = f32[2,8,4,128,1024]{4,3,2,1,0:T(8,128)} custom-call(s32[2]{0:T(128)} %pad_add_fusion.place, bf16[4,4,8,64,128]{4,3,2,1,0:T(8,128)(2,1)} %copy-done.3, bf16[4,4,8,64,128]{4,3,2,1,0:T(8,128)(2,1)} %all-to-all-done.1.refs_5_.refs_1_, bf16[4,4,8,64,128]{4,3,2,1,0:T(8,128)(2,1)} %all-to-all-done.2.refs_5_.refs_2_, ...), custom_call_target="tpu_custom_call" | custom-call | flops 25769803776 | bytes 33554432 | tf_op jit(solution)/shard_map/correlate/pallas_call | solution.py:247
  456.9 8.0 %all-to-all-done.7.refs_0_ = bf16[4,4,8,64,128]{4,3,2,1,0:T(8,128)(2,1)S(1)} async-done(((bf16[4,4,8,64,128]{4,3,2,1,0:T(8,128)(2,1)}), bf16[4,4,8,64,128]{4,3,2,1,0:T(8,128)(2,1)S(1)}, u32[]{:S(2)}, u32[]{:S(2)}) %all-to-all-start.7) | async-done | bytes 2097184 | tf_op jit(solution)/shard_map/all_to_all | solution.py:284
  466.3 4.4 collective-permute-done.31.refs_3_
  471.9 28.9 %correlate.3 = f32[2,8,4,128,1024]{4,3,2,1,0:T(8,128)} custom-call(s32[2]{0:T(128)} %pad_add_fusion.place, bf16[4,4,8,64,128]{4,3,2,1,0:T(8,128)(2,1)} %copy-done.1, bf16[4,4,8,64,128]{4,3,2,1,0:T(8,128)(2,1)} %after.1.refs_1_, bf16[4,4,8,64,128]{4,3,2,1,0:T(8,128)(2,1)} %collective-permute-done.30.refs_2_, ...), custom_call_target="tpu_custom_call", output_to_operand_aliasing={{}: (5, {})} | custom-call | flops 8589934592 | bytes 67108864 | tf_op jit(solution)/shard_map/correlate/pallas_call | solution.py:247
  (99 shorter events, 51.9 us)
Async XLA Ops:
  38.5 56.1 %collective-permute-start.6 = (bf16[1,4,8,64,128]{4,3,2,1,0:T(8,128)(2,1)}, bf16[1,4,8,64,128]{4,3,2,1,0:T(8,128)(2,1)}, u32[]{:S(2)}, u32[]{:S(2)}) collective-permute-start(bf16[1,4,8,64,128]{4,3,2,1,0:T(8,128)(2,1)} %get-tuple-element.46), channel_id=1, source_target_pairs={{0,6},{2,0},{4,2},{6,4},{1,7},{3,1},{5,3},{7,5},{8,14},{10,8},{12,... | collective-permute-start | bytes 1572872 | tf_op jit(solution)/shard_map/ppermute | solution.py:280
  40.8 53.9 %collective-permute-start.7 = (bf16[1,4,8,64,128]{4,3,2,1,0:T(8,128)(2,1)}, bf16[1,4,8,64,128]{4,3,2,1,0:T(8,128)(2,1)}, u32[]{:S(2)}, u32[]{:S(2)}) collective-permute-start(bf16[1,4,8,64,128]{4,3,2,1,0:T(8,128)(2,1)} %get-tuple-element.47), channel_id=1, source_target_pairs={{0,4},{2,6},{4,0},{6,2},{1,5},{3,7},{5,1},{7,3},{8,12},{10,14},{12... | collective-permute-start | bytes 1572872 | tf_op jit(solution)/shard_map/ppermute | solution.py:280
  42.4 52.3 %collective-permute-start.8 = (bf16[1,4,8,64,128]{4,3,2,1,0:T(8,128)(2,1)}, bf16[1,4,8,64,128]{4,3,2,1,0:T(8,128)(2,1)}, u32[]{:S(2)}, u32[]{:S(2)}) collective-permute-start(bf16[1,4,8,64,128]{4,3,2,1,0:T(8,128)(2,1)} %get-tuple-element.48), channel_id=1, source_target_pairs={{0,2},{2,4},{4,6},{6,0},{1,3},{3,5},{5,7},{7,1},{8,10},{10,12},{12... | collective-permute-start | bytes 1572872 | tf_op jit(solution)/shard_map/ppermute | solution.py:280
  51.1 49.9 %all-to-all-start = ((bf16[4,4,8,64,128]{4,3,2,1,0:T(8,128)(2,1)}), bf16[4,4,8,64,128]{4,3,2,1,0:T(8,128)(2,1)S(1)}, u32[]{:S(2)}, u32[]{:S(2)}) async-start(bf16[4,4,8,64,128]{4,3,2,1,0:T(8,128)(2,1)} %join.8.rest_0_), calls=%async_computation | async-start | bytes 4194304 | tf_op jit(solution)/shard_map/all_to_all | solution.py:284
  83.6 51.6 %collective-permute-start.3 = (bf16[2,4,8,64,128]{4,3,2,1,0:T(8,128)(2,1)}, bf16[2,4,8,64,128]{4,3,2,1,0:T(8,128)(2,1)S(1)}, u32[]{:S(2)}, u32[]{:S(2)}) collective-permute-start(bf16[2,4,8,64,128]{4,3,2,1,0:T(8,128)(2,1)} %get-tuple-element.43), channel_id=1, source_target_pairs={{0,6},{2,0},{4,2},{6,4},{1,7},{3,1},{5,3},{7,5},{8,14},{10,8},{12,... | collective-permute-start | bytes 3145736 | tf_op jit(solution)/shard_map/ppermute | solution.py:280
  101.0 52.2 %all-to-all-start.1 = ((bf16[4,4,8,64,128]{4,3,2,1,0:T(8,128)(2,1)}), bf16[4,4,8,64,128]{4,3,2,1,0:T(8,128)(2,1)}, u32[]{:S(2)}, u32[]{:S(2)}) async-start(bf16[4,4,8,64,128]{4,3,2,1,0:T(8,128)(2,1)} %join.9.rest_0_), calls=%async_computation.1 | async-start | bytes 4194304 | tf_op jit(solution)/shard_map/all_to_all | solution.py:284
  132.3 52.2 %collective-permute-start.12 = (bf16[2,4,8,64,128]{4,3,2,1,0:T(8,128)(2,1)}, bf16[2,4,8,64,128]{4,3,2,1,0:T(8,128)(2,1)}, u32[]{:S(2)}, u32[]{:S(2)}) collective-permute-start(bf16[2,4,8,64,128]{4,3,2,1,0:T(8,128)(2,1)} %get-tuple-element.54), channel_id=1, source_target_pairs={{0,6},{2,0},{4,2},{6,4},{1,7},{3,1},{5,3},{7,5},{8,14},{10,8},{12,... | collective-permute-start | bytes 3145736 | tf_op jit(solution)/shard_map/ppermute | solution.py:280
  134.5 50.6 %collective-permute-start.13 = (bf16[2,4,8,64,128]{4,3,2,1,0:T(8,128)(2,1)}, bf16[2,4,8,64,128]{4,3,2,1,0:T(8,128)(2,1)}, u32[]{:S(2)}, u32[]{:S(2)}) collective-permute-start(bf16[2,4,8,64,128]{4,3,2,1,0:T(8,128)(2,1)} %get-tuple-element.55), channel_id=1, source_target_pairs={{0,4},{2,6},{4,0},{6,2},{1,5},{3,7},{5,1},{7,3},{8,12},{10,14},{12... | collective-permute-start | bytes 3145736 | tf_op jit(solution)/shard_map/ppermute | solution.py:280
  135.3 51.8 %collective-permute-start.14 = (bf16[2,4,8,64,128]{4,3,2,1,0:T(8,128)(2,1)}, bf16[2,4,8,64,128]{4,3,2,1,0:T(8,128)(2,1)}, u32[]{:S(2)}, u32[]{:S(2)}) collective-permute-start(bf16[2,4,8,64,128]{4,3,2,1,0:T(8,128)(2,1)} %get-tuple-element.56), channel_id=1, source_target_pairs={{0,2},{2,4},{4,6},{6,0},{1,3},{3,5},{5,7},{7,1},{8,10},{10,12},{12... | collective-permute-start | bytes 3145736 | tf_op jit(solution)/shard_map/ppermute | solution.py:280
  135.3 51.7 %collective-permute-start.15 = (bf16[4,4,8,64,128]{4,3,2,1,0:T(8,128)(2,1)S(1)}, bf16[4,4,8,64,128]{4,3,2,1,0:T(8,128)(2,1)}, u32[]{:S(2)}, u32[]{:S(2)}) collective-permute-start(bf16[4,4,8,64,128]{4,3,2,1,0:T(8,128)(2,1)S(1)} %all-to-all-done.refs_5_.refs_0_), channel_id=1, source_target_pairs={{0,1},{1,0},{2,3},{3,2},{4,5},{5,4},{6,7},{7,6},{8,9},{9,8},{10,11... | collective-permute-start | bytes 6291464 | tf_op jit(solution)/shard_map/ppermute | solution.py:280
  153.2 52.2 %all-to-all-start.2 = ((bf16[4,4,8,64,128]{4,3,2,1,0:T(8,128)(2,1)}), bf16[4,4,8,64,128]{4,3,2,1,0:T(8,128)(2,1)}, u32[]{:S(2)}, u32[]{:S(2)}) async-start(bf16[4,4,8,64,128]{4,3,2,1,0:T(8,128)(2,1)} %join.10.rest_0_), calls=%async_computation.2 | async-start | bytes 4194304 | tf_op jit(solution)/shard_map/all_to_all | solution.py:284
  184.5 51.2 %collective-permute-start.9 = (bf16[2,4,8,64,128]{4,3,2,1,0:T(8,128)(2,1)}, bf16[2,4,8,64,128]{4,3,2,1,0:T(8,128)(2,1)S(1)}, u32[]{:S(2)}, u32[]{:S(2)}) collective-permute-start(bf16[2,4,8,64,128]{4,3,2,1,0:T(8,128)(2,1)} %get-tuple-element.51), channel_id=1, source_target_pairs={{0,6},{2,0},{4,2},{6,4},{1,7},{3,1},{5,3},{7,5},{8,14},{10,8},{12,... | collective-permute-start | bytes 3145736 | tf_op jit(solution)/shard_map/ppermute | solution.py:280
  184.5 51.8 %collective-permute-start.10 = (bf16[2,4,8,64,128]{4,3,2,1,0:T(8,128)(2,1)}, bf16[2,4,8,64,128]{4,3,2,1,0:T(8,128)(2,1)}, u32[]{:S(2)}, u32[]{:S(2)}) collective-permute-start(bf16[2,4,8,64,128]{4,3,2,1,0:T(8,128)(2,1)} %get-tuple-element.52), channel_id=1, source_target_pairs={{0,4},{2,6},{4,0},{6,2},{1,5},{3,7},{5,1},{7,3},{8,12},{10,14},{12... | collective-permute-start | bytes 3145736 | tf_op jit(solution)/shard_map/ppermute | solution.py:280
  185.1 53.2 %collective-permute-start.11 = (bf16[2,4,8,64,128]{4,3,2,1,0:T(8,128)(2,1)}, bf16[2,4,8,64,128]{4,3,2,1,0:T(8,128)(2,1)}, u32[]{:S(2)}, u32[]{:S(2)}) collective-permute-start(bf16[2,4,8,64,128]{4,3,2,1,0:T(8,128)(2,1)} %get-tuple-element.53), channel_id=1, source_target_pairs={{0,2},{2,4},{4,6},{6,0},{1,3},{3,5},{5,7},{7,1},{8,10},{10,12},{12... | collective-permute-start | bytes 3145736 | tf_op jit(solution)/shard_map/ppermute | solution.py:280
  187.0 51.2 %collective-permute-start.16 = (bf16[4,4,8,64,128]{4,3,2,1,0:T(8,128)(2,1)}, bf16[4,4,8,64,128]{4,3,2,1,0:T(8,128)(2,1)}, u32[]{:S(2)}, u32[]{:S(2)}) collective-permute-start(bf16[4,4,8,64,128]{4,3,2,1,0:T(8,128)(2,1)} %all-to-all-done.1.refs_5_.refs_1_), channel_id=1, source_target_pairs={{0,1},{1,0},{2,3},{3,2},{4,5},{5,4},{6,7},{7,6},{8,9},{9,8},{10,11... | collective-permute-start | bytes 6291464 | tf_op jit(solution)/shard_map/ppermute | solution.py:280
  205.4 51.3 %all-to-all-start.3 = ((bf16[4,4,8,64,128]{4,3,2,1,0:T(8,128)(2,1)}), bf16[4,4,8,64,128]{4,3,2,1,0:T(8,128)(2,1)S(1)}, u32[]{:S(2)}, u32[]{:S(2)}) async-start(bf16[4,4,8,64,128]{4,3,2,1,0:T(8,128)(2,1)} %join.11.rest_0_), calls=%async_computation.3 | async-start | bytes 4194304 | tf_op jit(solution)/shard_map/all_to_all | solution.py:284
  235.7 52.2 %collective-permute-start.20 = (bf16[2,4,8,64,128]{4,3,2,1,0:T(8,128)(2,1)}, bf16[2,4,8,64,128]{4,3,2,1,0:T(8,128)(2,1)}, u32[]{:S(2)}, u32[]{:S(2)}) collective-permute-start(bf16[2,4,8,64,128]{4,3,2,1,0:T(8,128)(2,1)} %get-tuple-element.62), channel_id=1, source_target_pairs={{0,6},{2,0},{4,2},{6,4},{1,7},{3,1},{5,3},{7,5},{8,14},{10,8},{12,... | collective-permute-start | bytes 3145736 | tf_op jit(solution)/shard_map/ppermute | solution.py:280
  235.7 52.7 %collective-permute-start.21 = (bf16[2,4,8,64,128]{4,3,2,1,0:T(8,128)(2,1)}, bf16[2,4,8,64,128]{4,3,2,1,0:T(8,128)(2,1)}, u32[]{:S(2)}, u32[]{:S(2)}) collective-permute-start(bf16[2,4,8,64,128]{4,3,2,1,0:T(8,128)(2,1)} %get-tuple-element.63), channel_id=1, source_target_pairs={{0,4},{2,6},{4,0},{6,2},{1,5},{3,7},{5,1},{7,3},{8,12},{10,14},{12... | collective-permute-start | bytes 3145736 | tf_op jit(solution)/shard_map/ppermute | solution.py:280
  236.3 54.1 %collective-permute-start.22 = (bf16[2,4,8,64,128]{4,3,2,1,0:T(8,128)(2,1)}, bf16[2,4,8,64,128]{4,3,2,1,0:T(8,128)(2,1)}, u32[]{:S(2)}, u32[]{:S(2)}) collective-permute-start(bf16[2,4,8,64,128]{4,3,2,1,0:T(8,128)(2,1)} %get-tuple-element.64), channel_id=1, source_target_pairs={{0,2},{2,4},{4,6},{6,0},{1,3},{3,5},{5,7},{7,1},{8,10},{10,12},{12... | collective-permute-start | bytes 3145736 | tf_op jit(solution)/shard_map/ppermute | solution.py:280
  238.3 52.1 %collective-permute-start.23 = (bf16[4,4,8,64,128]{4,3,2,1,0:T(8,128)(2,1)}, bf16[4,4,8,64,128]{4,3,2,1,0:T(8,128)(2,1)}, u32[]{:S(2)}, u32[]{:S(2)}) collective-permute-start(bf16[4,4,8,64,128]{4,3,2,1,0:T(8,128)(2,1)} %all-to-all-done.2.refs_5_.refs_2_), channel_id=1, source_target_pairs={{0,1},{1,0},{2,3},{3,2},{4,5},{5,4},{6,7},{7,6},{8,9},{9,8},{10,11... | collective-permute-start | bytes 6291464 | tf_op jit(solution)/shard_map/ppermute | solution.py:280
  256.7 52.2 %all-to-all-start.4 = ((bf16[4,4,8,64,128]{4,3,2,1,0:T(8,128)(2,1)}), bf16[4,4,8,64,128]{4,3,2,1,0:T(8,128)(2,1)}, u32[]{:S(2)}, u32[]{:S(2)}) async-start(bf16[4,4,8,64,128]{4,3,2,1,0:T(8,128)(2,1)} %join.12.rest_0_), calls=%async_computation.4 | async-start | bytes 4194304 | tf_op jit(solution)/shard_map/all_to_all | solution.py:284
  287.8 52.2 %collective-permute-start.17 = (bf16[2,4,8,64,128]{4,3,2,1,0:T(8,128)(2,1)}, bf16[2,4,8,64,128]{4,3,2,1,0:T(8,128)(2,1)S(1)}, u32[]{:S(2)}, u32[]{:S(2)}) collective-permute-start(bf16[2,4,8,64,128]{4,3,2,1,0:T(8,128)(2,1)} %get-tuple-element.59), channel_id=1, source_target_pairs={{0,6},{2,0},{4,2},{6,4},{1,7},{3,1},{5,3},{7,5},{8,14},{10,8},{12,... | collective-permute-start | bytes 3145736 | tf_op jit(solution)/shard_map/ppermute | solution.py:280
  287.9 52.8 %collective-permute-start.18 = (bf16[2,4,8,64,128]{4,3,2,1,0:T(8,128)(2,1)}, bf16[2,4,8,64,128]{4,3,2,1,0:T(8,128)(2,1)}, u32[]{:S(2)}, u32[]{:S(2)}) collective-permute-start(bf16[2,4,8,64,128]{4,3,2,1,0:T(8,128)(2,1)} %get-tuple-element.60), channel_id=1, source_target_pairs={{0,4},{2,6},{4,0},{6,2},{1,5},{3,7},{5,1},{7,3},{8,12},{10,14},{12... | collective-permute-start | bytes 3145736 | tf_op jit(solution)/shard_map/ppermute | solution.py:280
  288.4 54.2 %collective-permute-start.19 = (bf16[2,4,8,64,128]{4,3,2,1,0:T(8,128)(2,1)}, bf16[2,4,8,64,128]{4,3,2,1,0:T(8,128)(2,1)}, u32[]{:S(2)}, u32[]{:S(2)}) collective-permute-start(bf16[2,4,8,64,128]{4,3,2,1,0:T(8,128)(2,1)} %get-tuple-element.61), channel_id=1, source_target_pairs={{0,2},{2,4},{4,6},{6,0},{1,3},{3,5},{5,7},{7,1},{8,10},{10,12},{12... | collective-permute-start | bytes 3145736 | tf_op jit(solution)/shard_map/ppermute | solution.py:280
  290.4 52.2 %collective-permute-start.24 = (bf16[4,4,8,64,128]{4,3,2,1,0:T(8,128)(2,1)S(1)}, bf16[4,4,8,64,128]{4,3,2,1,0:T(8,128)(2,1)}, u32[]{:S(2)}, u32[]{:S(2)}) collective-permute-start(bf16[4,4,8,64,128]{4,3,2,1,0:T(8,128)(2,1)S(1)} %all-to-all-done.3.refs_5_.refs_3_), channel_id=1, source_target_pairs={{0,1},{1,0},{2,3},{3,2},{4,5},{5,4},{6,7},{7,6},{8,9},{9,8},{10,11... | collective-permute-start | bytes 6291464 | tf_op jit(solution)/shard_map/ppermute | solution.py:280
  308.9 52.2 %all-to-all-start.6 = ((bf16[4,4,8,64,128]{4,3,2,1,0:T(8,128)(2,1)}), bf16[4,4,8,64,128]{4,3,2,1,0:T(8,128)(2,1)}, u32[]{:S(2)}, u32[]{:S(2)}) async-start(bf16[4,4,8,64,128]{4,3,2,1,0:T(8,128)(2,1)} %join.13.rest_0_), calls=%async_computation.6 | async-start | bytes 4194304 | tf_op jit(solution)/shard_map/all_to_all | solution.py:284
  340.1 47.0 %collective-permute-start.26 = (bf16[2,4,8,64,128]{4,3,2,1,0:T(8,128)(2,1)}, bf16[2,4,8,64,128]{4,3,2,1,0:T(8,128)(2,1)}, u32[]{:S(2)}, u32[]{:S(2)}) collective-permute-start(bf16[2,4,8,64,128]{4,3,2,1,0:T(8,128)(2,1)} %get-tuple-element.67), channel_id=1, source_target_pairs={{0,4},{2,6},{4,0},{6,2},{1,5},{3,7},{5,1},{7,3},{8,12},{10,14},{12... | collective-permute-start | bytes 3145736 | tf_op jit(solution)/shard_map/ppermute | solution.py:280
  340.7 46.4 %collective-permute-start.27 = (bf16[2,4,8,64,128]{4,3,2,1,0:T(8,128)(2,1)}, bf16[2,4,8,64,128]{4,3,2,1,0:T(8,128)(2,1)}, u32[]{:S(2)}, u32[]{:S(2)}) collective-permute-start(bf16[2,4,8,64,128]{4,3,2,1,0:T(8,128)(2,1)} %get-tuple-element.68), channel_id=1, source_target_pairs={{0,2},{2,4},{4,6},{6,0},{1,3},{3,5},{5,7},{7,1},{8,10},{10,12},{12... | collective-permute-start | bytes 3145736 | tf_op jit(solution)/shard_map/ppermute | solution.py:280
  361.1 51.3 %all-to-all-start.5 = ((bf16[4,4,8,64,128]{4,3,2,1,0:T(8,128)(2,1)}), bf16[4,4,8,64,128]{4,3,2,1,0:T(8,128)(2,1)S(1)}, u32[]{:S(2)}, u32[]{:S(2)}) async-start(bf16[4,4,8,64,128]{4,3,2,1,0:T(8,128)(2,1)} %join.14.refs_4_), calls=%async_computation.5 | async-start | bytes 4194304 | tf_op jit(solution)/shard_map/all_to_all | solution.py:284
  364.7 52.9 %collective-permute-start.29 = (bf16[4,4,8,64,128]{4,3,2,1,0:T(8,128)(2,1)}, bf16[4,4,8,64,128]{4,3,2,1,0:T(8,128)(2,1)}, u32[]{:S(2)}, u32[]{:S(2)}) collective-permute-start(bf16[4,4,8,64,128]{4,3,2,1,0:T(8,128)(2,1)} %all-to-all-done.6.refs_5_), channel_id=1, source_target_pairs={{0,1},{1,0},{2,3},{3,2},{4,5},{5,4},{6,7},{7,6},{8,9},{9,8},{10,11... | collective-permute-start | bytes 6291464 | tf_op jit(solution)/shard_map/ppermute | solution.py:280
  413.6 51.3 %all-to-all-start.7 = ((bf16[4,4,8,64,128]{4,3,2,1,0:T(8,128)(2,1)}), bf16[4,4,8,64,128]{4,3,2,1,0:T(8,128)(2,1)S(1)}, u32[]{:S(2)}, u32[]{:S(2)}) async-start(bf16[4,4,8,64,128]{4,3,2,1,0:T(8,128)(2,1)} %join.15), calls=%async_computation.7 | async-start | bytes 4194304 | tf_op jit(solution)/shard_map/all_to_all | solution.py:284
  417.5 48.8 %collective-permute-start.30 = (bf16[4,4,8,64,128]{4,3,2,1,0:T(8,128)(2,1)}, bf16[4,4,8,64,128]{4,3,2,1,0:T(8,128)(2,1)}, u32[]{:S(2)}, u32[]{:S(2)}) collective-permute-start(bf16[4,4,8,64,128]{4,3,2,1,0:T(8,128)(2,1)} %copy-done.1), channel_id=1, source_target_pairs={{0,1},{1,0},{2,3},{3,2},{4,5},{5,4},{6,7},{7,6},{8,9},{9,8},{10,11... | collective-permute-start | bytes 6291464 | tf_op jit(solution)/shard_map/ppermute | solution.py:280
  (21 other events, 328.2 us)
